TPU v7x, 512 devices: a whole 4x4x16 slice. The times are simulated.
512 devices in a mesh: gx: 32 (over x, y, core), gy: 16 (over z).
Axes of the slice: x: 4, y: 4, z: 16, core: 2. Of those that a mesh axis runs over, the one named last changes fastest.
Arguments:
- basis_vec: float32 [16, 512, 4096], P(None, 'gx', 'gy'), may hold values from -6 to 6
- conductivity: float32 [16, 512, 4096], P(None, 'gx', 'gy'), may hold values from 0.2 to 5
- sign_vals: int32 [512, 4096], P('gx', 'gy'), may hold values from -1 to 1, as said below
- sample_cols: int32 [256], P('gy'), may hold values from 0 to 255, as said below
Outputs:
- precond: float32 [16, 512, 4096], P(None, 'gx', 'gy')
- image_vec: float32 [16, 512, 4096], P(None, 'gx', 'gy')
- sketch: float32 [16, 512, 16], P(None, 'gx')
Inputs may be any that keep to these rules, and one draw needn't show every extreme that they name: `sign_vals`: each entry is -1 or 1. `sample_cols`: the entries of each aligned block of 16 are distinct column offsets within one block of 256 columns.
All inputs are finite; a program needn't handle non-finite values.
Results may differ from a plain program's by a relative error of at most 0.0002.
Values sent between devices are 32-bit elements; how exact they have to be, the bound alone decides.
A program may use at most 64 MiB of HBM per device.

v0:
```python
import jax
import jax.numpy as jnp
from jax import lax
from jax.sharding import PartitionSpec as P

SWEEPS = 8
reaction = 0.5
lowest = 0.5
highest = 62.0
half_root = 0.7071067811865476


def extended(array, sides, width):
    for axis, dim in sides:
        devices, length = (lax.axis_size(axis), array.shape[dim])
        up = [(i, (i + 1) % devices) for i in range(devices - 1)]
        down = [(j, i) for i, j in up]
        last = lax.slice_in_dim(array, length - width, length, axis=dim)
        leading = lax.slice_in_dim(array, 0, width, axis=dim)
        before = lax.ppermute(last, axis, up)
        after = lax.ppermute(leading, axis, down)
        array = jnp.concatenate([before, array, after], axis=dim)
    return array


def partner_2(array, axis, stride):
    return lax.ppermute(array, axis, [(i, i ^ 1 << stride) for i in range(lax.axis_size(axis))])


def operate(values, conduct):
    padded = jnp.pad(values, ((1, 1), (0, 0), (0, 0)))
    centre_val = padded[1:-1, 1:-1, 1:-1]
    kappa_mid = conduct[1:-1, 1:-1, 1:-1]
    neighbours = (
        (padded[2:, 1:-1, 1:-1], conduct[2:, 1:-1, 1:-1]),
        (padded[:-2, 1:-1, 1:-1], conduct[:-2, 1:-1, 1:-1]),
        (padded[1:-1, 2:, 1:-1], conduct[1:-1, 2:, 1:-1]),
        (padded[1:-1, :-2, 1:-1], conduct[1:-1, :-2, 1:-1]),
        (padded[1:-1, 1:-1, 2:], conduct[1:-1, 1:-1, 2:]),
        (padded[1:-1, 1:-1, :-2], conduct[1:-1, 1:-1, :-2]),
    )
    summed = reaction * centre_val
    for near_value, near_kappa in neighbours:
        summed = summed + 0.5 * (kappa_mid + near_kappa) * (centre_val - near_value)
    return summed


def hartley_table(length):
    row_ids = jnp.arange(length, dtype=jnp.int32)[:, None]
    col_ids = jnp.arange(length, dtype=jnp.int32)[None, :]
    angles = (row_ids * col_ids % length).astype(jnp.float32) * (2.0 * jnp.pi / length)
    return (jnp.cos(angles) + jnp.sin(angles)) / jnp.sqrt(jnp.float32(length))


def per_device(basis_vec, conductivity, sign_vals, sample_cols):
    depth_cells, row_cells, col_cells = basis_vec.shape
    margin = 1
    conduct = extended(conductivity, (("gx", 1), ("gy", 2)), margin)
    conduct = jnp.pad(conduct, ((1, 1), (0, 0), (0, 0)))
    conduct_one = conduct

    def apply_rim(values):
        padded = extended(values, (("gx", 1), ("gy", 2)), 1)
        return operate(padded, conduct_one)

    middle = (highest + lowest) / 2.0
    spread = (highest - lowest) / 2.0
    sig_ratio = middle / spread
    rho_now = 1.0 / sig_ratio
    residual = basis_vec
    direction = residual * (1.0 / middle)
    precond = jnp.zeros_like(basis_vec)
    for sweep_no in range(SWEEPS):
        precond = precond + direction
        if sweep_no < SWEEPS - 1:
            residual = residual - apply_rim(direction)
            rho_next = 1.0 / (2.0 * sig_ratio - rho_now)
            direction = rho_next * rho_now * direction + 2.0 * rho_next / spread * residual
            rho_now = rho_next
    image_vec = apply_rim(precond)
    flipped = image_vec * sign_vals.astype(jnp.float32)[None]
    hartley_mat = hartley_table(row_cells)
    current = jnp.einsum("jk,dkc->djc", hartley_mat, flipped, precision=lax.Precision.HIGHEST)
    for section_bit in range(lax.axis_size("gx").bit_length() - 1):
        partner = partner_2(current, "gx", section_bit)
        upper_half = lax.axis_index("gx") >> section_bit & 1 == 1
        current = jnp.where(upper_half, partner - current, current + partner) * half_root
    picked = jnp.take(current, sample_cols, axis=2)
    sketch = lax.psum(picked, "gy")
    return (precond, image_vec, sketch)


def solution(mesh):
    in_specs = (P(None, "gx", "gy"), P(None, "gx", "gy"), P("gx", "gy"), P("gy"))
    out_specs = (P(None, "gx", "gy"), P(None, "gx", "gy"), P(None, "gx", None))
    return jax.shard_map(
        per_device, mesh=mesh, in_specs=in_specs, out_specs=out_specs, check_vma=False
    )
```

profile of v0, /device:TPU:18, one launch (start us, length us, event | category | flops | bytes accessed | tf_op | source)
XLA Modules:
  0.0 297.3 jit_solution(12451882532741742519)
XLA Ops:
  1.7 1.9 collective-permute-start
  3.6 3.6 %collective-permute-start.1 = (f32[16,1,256]{2,1,0:T(1,128)S(1)}, f32[16,1,256]{2,1,0:T(1,128)S(1)}, u32[]{:S(2)}, u32[]{:S(2)}) collective-permute-start(f32[16,1,256]{2,1,0:T(1,128)S(1)} %get-tuple-element.54), channel_id=1, source_target_pairs={{16,0},{32,16},{48,32},{64,48},{80,64},{96,80},{112,96},{128,112},... | collective-permute-start | bytes 49160 | tf_op jit(solution)/shard_map/ppermute | solution.py:21
  8.3 1.9 collective-permute-start.4
  10.2 3.6 %collective-permute-start.5 = (f32[16,1,256]{2,1,0:T(1,128)S(1)}, f32[16,1,256]{2,1,0:T(1,128)S(1)}, u32[]{:S(2)}, u32[]{:S(2)}) collective-permute-start(f32[16,1,256]{2,1,0:T(1,128)S(1)} %get-tuple-element.57), channel_id=1, source_target_pairs={{16,0},{32,16},{48,32},{64,48},{80,64},{96,80},{112,96},{128,112},... | collective-permute-start | bytes 49160 | tf_op jit(solution)/shard_map/ppermute | solution.py:21
  15.0 4.0 %collective-permute-start.2 = (f32[16,18,1]{2,1,0:T(8,128)S(1)}, f32[16,18,1]{2,1,0:T(8,128)S(1)}, u32[]{:S(2)}, u32[]{:S(2)}) collective-permute-start(f32[16,18,1]{2,1,0:T(8,128)S(1)} %get-tuple-element.36), channel_id=1, source_target_pairs={{0,1},{1,2},{2,3},{3,4},{4,5},{5,6},{6,7},{7,8},{8,9},{9,10},{10,1... | collective-permute-start | bytes 3464 | tf_op jit(solution)/shard_map/ppermute | solution.py:20
  20.5 4.6 %collective-permute-start.6 = (f32[16,18,1]{2,1,0:T(8,128)S(1)}, f32[16,18,1]{2,1,0:T(8,128)S(1)}, u32[]{:S(2)}, u32[]{:S(2)}) collective-permute-start(f32[16,18,1]{2,1,0:T(8,128)S(1)} %get-tuple-element.39), channel_id=1, source_target_pairs={{0,1},{1,2},{2,3},{3,4},{4,5},{5,6},{6,7},{7,8},{8,9},{9,10},{10,1... | collective-permute-start | bytes 3464 | tf_op jit(solution)/shard_map/ppermute | solution.py:20
  28.6 4.3 %collective-permute-done.7 = f32[16,18,1]{2,1,0:T(8,128)S(1)} collective-permute-done((f32[16,18,1]{2,1,0:T(8,128)S(1)}, f32[16,18,1]{2,1,0:T(8,128)S(1)}, u32[]{:S(2)}, u32[]{:S(2)}) %collective-permute-start.7) | collective-permute-done | bytes 1184 | tf_op jit(solution)/shard_map/ppermute | solution.py:21
  34.2 1.9 collective-permute-start.8
  36.2 3.6 %collective-permute-start.9 = (f32[16,1,256]{2,1,0:T(1,128)S(1)}, f32[16,1,256]{2,1,0:T(1,128)S(1)}, u32[]{:S(2)}, u32[]{:S(2)}) collective-permute-start(f32[16,1,256]{2,1,0:T(1,128)S(1)} %get-tuple-element.53), channel_id=1, source_target_pairs={{16,0},{32,16},{48,32},{64,48},{80,64},{96,80},{112,96},{128,112},... | collective-permute-start | bytes 49160 | tf_op jit(solution)/shard_map/ppermute | solution.py:21
  41.9 4.7 %collective-permute-start.10 = (f32[16,18,1]{2,1,0:T(8,128)S(1)}, f32[16,18,1]{2,1,0:T(8,128)S(1)}, u32[]{:S(2)}, u32[]{:S(2)}) collective-permute-start(f32[16,18,1]{2,1,0:T(8,128)S(1)} %get-tuple-element.35), channel_id=1, source_target_pairs={{0,1},{1,2},{2,3},{3,4},{4,5},{5,6},{6,7},{7,8},{8,9},{9,10},{10,1... | collective-permute-start | bytes 3464 | tf_op jit(solution)/shard_map/ppermute | solution.py:20
  47.9 2.4 collective-permute-done.10
  50.3 5.8 %collective-permute-done.11 = f32[16,18,1]{2,1,0:T(8,128)S(1)} collective-permute-done((f32[16,18,1]{2,1,0:T(8,128)S(1)}, f32[16,18,1]{2,1,0:T(8,128)S(1)}, u32[]{:S(2)}, u32[]{:S(2)}) %collective-permute-start.11) | collective-permute-done | bytes 1184 | tf_op jit(solution)/shard_map/ppermute | solution.py:21
  57.2 3.3 %collective-permute-start.12 = (f32[16,1,256]{2,1,0:T(1,128)S(1)}, f32[16,1,256]{2,1,0:T(1,128)S(1)}, u32[]{:S(2)}, u32[]{:S(2)}) collective-permute-start(f32[16,1,256]{2,1,0:T(1,128)S(1)} %get-tuple-element.50), channel_id=1, source_target_pairs={{0,16},{16,32},{32,48},{48,64},{64,80},{80,96},{96,112},{112,128},... | collective-permute-start | bytes 49160 | tf_op jit(solution)/shard_map/ppermute | solution.py:20
  60.5 2.3 collective-permute-start.13
  64.8 5.1 %collective-permute-start.14 = (f32[16,18,1]{2,1,0:T(8,128)S(1)}, f32[16,18,1]{2,1,0:T(8,128)S(1)}, u32[]{:S(2)}, u32[]{:S(2)}) collective-permute-start(f32[16,18,1]{2,1,0:T(8,128)S(1)} %get-tuple-element.33), channel_id=1, source_target_pairs={{0,1},{1,2},{2,3},{3,4},{4,5},{5,6},{6,7},{7,8},{8,9},{9,10},{10,1... | collective-permute-start | bytes 3464 | tf_op jit(solution)/shard_map/ppermute | solution.py:20
  73.1 4.4 %collective-permute-done.15 = f32[16,18,1]{2,1,0:T(8,128)S(1)} collective-permute-done((f32[16,18,1]{2,1,0:T(8,128)S(1)}, f32[16,18,1]{2,1,0:T(8,128)S(1)}, u32[]{:S(2)}, u32[]{:S(2)}) %collective-permute-start.15) | collective-permute-done | bytes 1184 | tf_op jit(solution)/shard_map/ppermute | solution.py:21
  78.5 4.7 %collective-permute-start.16 = (f32[16,1,256]{2,1,0:T(1,128)S(1)}, f32[16,1,256]{2,1,0:T(1,128)S(1)}, u32[]{:S(2)}, u32[]{:S(2)}) collective-permute-start(f32[16,1,256]{2,1,0:T(1,128)S(1)} %get-tuple-element.48), channel_id=1, source_target_pairs={{0,16},{16,32},{32,48},{48,64},{64,80},{80,96},{96,112},{112,128},... | collective-permute-start | bytes 49160 | tf_op jit(solution)/shard_map/ppermute | solution.py:20
  83.2 1.9 collective-permute-start.17
  85.1 2.5 collective-permute-done.17
  87.8 3.9 %collective-permute-start.18 = (f32[16,18,1]{2,1,0:T(8,128)S(1)}, f32[16,18,1]{2,1,0:T(8,128)S(1)}, u32[]{:S(2)}, u32[]{:S(2)}) collective-permute-start(f32[16,18,1]{2,1,0:T(8,128)S(1)} %get-tuple-element.31), channel_id=1, source_target_pairs={{0,1},{1,2},{2,3},{3,4},{4,5},{5,6},{6,7},{7,8},{8,9},{9,10},{10,1... | collective-permute-start | bytes 3464 | tf_op jit(solution)/shard_map/ppermute | solution.py:20
  94.9 4.4 %collective-permute-done.19 = f32[16,18,1]{2,1,0:T(8,128)S(1)} collective-permute-done((f32[16,18,1]{2,1,0:T(8,128)S(1)}, f32[16,18,1]{2,1,0:T(8,128)S(1)}, u32[]{:S(2)}, u32[]{:S(2)}) %collective-permute-start.19) | collective-permute-done | bytes 1184 | tf_op jit(solution)/shard_map/ppermute | solution.py:21
  100.3 4.5 %collective-permute-start.20 = (f32[16,1,256]{2,1,0:T(1,128)S(1)}, f32[16,1,256]{2,1,0:T(1,128)S(1)}, u32[]{:S(2)}, u32[]{:S(2)}) collective-permute-start(f32[16,1,256]{2,1,0:T(1,128)S(1)} %get-tuple-element.46), channel_id=1, source_target_pairs={{0,16},{16,32},{32,48},{48,64},{64,80},{80,96},{96,112},{112,128},... | collective-permute-start | bytes 49160 | tf_op jit(solution)/shard_map/ppermute | solution.py:20
  104.9 1.9 collective-permute-start.21
  106.8 2.6 collective-permute-done.21
  109.6 4.7 %collective-permute-start.22 = (f32[16,18,1]{2,1,0:T(8,128)S(1)}, f32[16,18,1]{2,1,0:T(8,128)S(1)}, u32[]{:S(2)}, u32[]{:S(2)}) collective-permute-start(f32[16,18,1]{2,1,0:T(8,128)S(1)} %get-tuple-element.29), channel_id=1, source_target_pairs={{0,1},{1,2},{2,3},{3,4},{4,5},{5,6},{6,7},{7,8},{8,9},{9,10},{10,1... | collective-permute-start | bytes 3464 | tf_op jit(solution)/shard_map/ppermute | solution.py:20
  117.5 4.4 %collective-permute-done.23 = f32[16,18,1]{2,1,0:T(8,128)S(1)} collective-permute-done((f32[16,18,1]{2,1,0:T(8,128)S(1)}, f32[16,18,1]{2,1,0:T(8,128)S(1)}, u32[]{:S(2)}, u32[]{:S(2)}) %collective-permute-start.23) | collective-permute-done | bytes 1184 | tf_op jit(solution)/shard_map/ppermute | solution.py:21
  122.9 4.9 %collective-permute-start.24 = (f32[16,1,256]{2,1,0:T(1,128)S(1)}, f32[16,1,256]{2,1,0:T(1,128)S(1)}, u32[]{:S(2)}, u32[]{:S(2)}) collective-permute-start(f32[16,1,256]{2,1,0:T(1,128)S(1)} %get-tuple-element.44), channel_id=1, source_target_pairs={{0,16},{16,32},{32,48},{48,64},{64,80},{80,96},{96,112},{112,128},... | collective-permute-start | bytes 49160 | tf_op jit(solution)/shard_map/ppermute | solution.py:20
  129.8 2.2 collective-permute-done.25
  132.2 5.1 %collective-permute-start.26 = (f32[16,18,1]{2,1,0:T(8,128)S(1)}, f32[16,18,1]{2,1,0:T(8,128)S(1)}, u32[]{:S(2)}, u32[]{:S(2)}) collective-permute-start(f32[16,18,1]{2,1,0:T(8,128)S(1)} %get-tuple-element.27), channel_id=1, source_target_pairs={{0,1},{1,2},{2,3},{3,4},{4,5},{5,6},{6,7},{7,8},{8,9},{9,10},{10,1... | collective-permute-start | bytes 3464 | tf_op jit(solution)/shard_map/ppermute | solution.py:20
  140.5 4.4 %collective-permute-done.27 = f32[16,18,1]{2,1,0:T(8,128)S(1)} collective-permute-done((f32[16,18,1]{2,1,0:T(8,128)S(1)}, f32[16,18,1]{2,1,0:T(8,128)S(1)}, u32[]{:S(2)}, u32[]{:S(2)}) %collective-permute-start.27) | collective-permute-done | bytes 1184 | tf_op jit(solution)/shard_map/ppermute | solution.py:21
  146.0 4.7 %collective-permute-start.28 = (f32[16,1,256]{2,1,0:T(1,128)S(1)}, f32[16,1,256]{2,1,0:T(1,128)S(1)}, u32[]{:S(2)}, u32[]{:S(2)}) collective-permute-start(f32[16,1,256]{2,1,0:T(1,128)S(1)} %get-tuple-element.42), channel_id=1, source_target_pairs={{0,16},{16,32},{32,48},{48,64},{64,80},{80,96},{96,112},{112,128},... | collective-permute-start | bytes 49160 | tf_op jit(solution)/shard_map/ppermute | solution.py:20
  152.6 2.5 collective-permute-done.29
  155.3 3.9 %collective-permute-start.30 = (f32[16,18,1]{2,1,0:T(8,128)S(1)}, f32[16,18,1]{2,1,0:T(8,128)S(1)}, u32[]{:S(2)}, u32[]{:S(2)}) collective-permute-start(f32[16,18,1]{2,1,0:T(8,128)S(1)} %get-tuple-element.25), channel_id=1, source_target_pairs={{0,1},{1,2},{2,3},{3,4},{4,5},{5,6},{6,7},{7,8},{8,9},{9,10},{10,1... | collective-permute-start | bytes 3464 | tf_op jit(solution)/shard_map/ppermute | solution.py:20
  162.4 4.4 %collective-permute-done.31 = f32[16,18,1]{2,1,0:T(8,128)S(1)} collective-permute-done((f32[16,18,1]{2,1,0:T(8,128)S(1)}, f32[16,18,1]{2,1,0:T(8,128)S(1)}, u32[]{:S(2)}, u32[]{:S(2)}) %collective-permute-start.31) | collective-permute-done | bytes 1184 | tf_op jit(solution)/shard_map/ppermute | solution.py:21
  167.9 4.7 %collective-permute-start.32 = (f32[16,1,256]{2,1,0:T(1,128)S(1)}, f32[16,1,256]{2,1,0:T(1,128)S(1)}, u32[]{:S(2)}, u32[]{:S(2)}) collective-permute-start(f32[16,1,256]{2,1,0:T(1,128)S(1)} %get-tuple-element.40), channel_id=1, source_target_pairs={{0,16},{16,32},{32,48},{48,64},{64,80},{80,96},{96,112},{112,128},... | collective-permute-start | bytes 49160 | tf_op jit(solution)/shard_map/ppermute | solution.py:20
  174.5 2.5 collective-permute-done.33
  177.2 3.9 %collective-permute-start.34 = (f32[16,18,1]{2,1,0:T(8,128)S(1)}, f32[16,18,1]{2,1,0:T(8,128)S(1)}, u32[]{:S(2)}, u32[]{:S(2)}) collective-permute-start(f32[16,18,1]{2,1,0:T(8,128)S(1)} %get-tuple-element.23), channel_id=1, source_target_pairs={{0,1},{1,2},{2,3},{3,4},{4,5},{5,6},{6,7},{7,8},{8,9},{9,10},{10,1... | collective-permute-start | bytes 3464 | tf_op jit(solution)/shard_map/ppermute | solution.py:20
  184.3 4.4 %collective-permute-done.35 = f32[16,18,1]{2,1,0:T(8,128)S(1)} collective-permute-done((f32[16,18,1]{2,1,0:T(8,128)S(1)}, f32[16,18,1]{2,1,0:T(8,128)S(1)}, u32[]{:S(2)}, u32[]{:S(2)}) %collective-permute-start.35) | collective-permute-done | bytes 1184 | tf_op jit(solution)/shard_map/ppermute | solution.py:21
  190.1 4.4 %collective-permute-start.36 = (f32[16,16,256]{2,1,0:T(8,128)S(1)}, f32[16,16,256]{2,1,0:T(8,128)S(1)}, u32[]{:S(2)}, u32[]{:S(2)}) collective-permute-start(f32[16,16,256]{2,1,0:T(8,128)S(1)} %convolution_bitcast_fusion), channel_id=1, source_target_pairs={{0,16},{16,0},{32,48},{48,32},{64,80},{80,64},{96,112},{112,96},{1... | collective-permute-start | bytes 786440 | tf_op jit(solution)/shard_map/ppermute | solution.py:27
  195.7 7.1 %collective-permute-start.37 = (f32[16,16,256]{2,1,0:T(8,128)S(1)}, f32[16,16,256]{2,1,0:T(8,128)S(1)}, u32[]{:S(2)}, u32[]{:S(2)}) collective-permute-start(f32[16,16,256]{2,1,0:T(8,128)S(1)} %select_multiply_fusion.4), channel_id=1, source_target_pairs={{0,32},{16,48},{32,0},{48,16},{64,96},{80,112},{96,64},{112,80},{1... | collective-permute-start | bytes 786440 | tf_op jit(solution)/shard_map/ppermute | solution.py:27
  202.8 6.8 %collective-permute-done.37 = f32[16,16,256]{2,1,0:T(8,128)S(1)} collective-permute-done((f32[16,16,256]{2,1,0:T(8,128)S(1)}, f32[16,16,256]{2,1,0:T(8,128)S(1)}, u32[]{:S(2)}, u32[]{:S(2)}) %collective-permute-start.37) | collective-permute-done | bytes 262176 | tf_op jit(solution)/shard_map/ppermute | solution.py:27
  209.6 3.0 %collective-permute-start.38 = (f32[16,16,256]{2,1,0:T(8,128)S(1)}, f32[16,16,256]{2,1,0:T(8,128)S(1)}, u32[]{:S(2)}, u32[]{:S(2)}) collective-permute-start(f32[16,16,256]{2,1,0:T(8,128)S(1)} %select_multiply_fusion.3), channel_id=1, source_target_pairs={{0,64},{16,80},{32,96},{48,112},{64,0},{80,16},{96,32},{112,48},{1... | collective-permute-start | bytes 786440 | tf_op jit(solution)/shard_map/ppermute | solution.py:27
  212.7 8.4 %collective-permute-done.38 = f32[16,16,256]{2,1,0:T(8,128)S(1)} collective-permute-done((f32[16,16,256]{2,1,0:T(8,128)S(1)}, f32[16,16,256]{2,1,0:T(8,128)S(1)}, u32[]{:S(2)}, u32[]{:S(2)}) %collective-permute-start.38) | collective-permute-done | bytes 262176 | tf_op jit(solution)/shard_map/ppermute | solution.py:27
  221.1 2.4 collective-permute-start.39
  223.6 6.5 %collective-permute-done.39 = f32[16,16,256]{2,1,0:T(8,128)S(1)} collective-permute-done((f32[16,16,256]{2,1,0:T(8,128)S(1)}, f32[16,16,256]{2,1,0:T(8,128)S(1)}, u32[]{:S(2)}, u32[]{:S(2)}) %collective-permute-start.39) | collective-permute-done | bytes 262176 | tf_op jit(solution)/shard_map/ppermute | solution.py:27
  230.2 2.8 collective-permute-start.40
  233.1 6.9 %collective-permute-done.40 = f32[16,16,256]{2,1,0:T(8,128)S(1)} collective-permute-done((f32[16,16,256]{2,1,0:T(8,128)S(1)}, f32[16,16,256]{2,1,0:T(8,128)S(1)}, u32[]{:S(2)}, u32[]{:S(2)}) %collective-permute-start.40) | collective-permute-done | bytes 262176 | tf_op jit(solution)/shard_map/ppermute | solution.py:27
  242.0 54.6 %psum.7 = f32[16,16,16]{1,0,2:T(8,128)S(1)} all-reduce(f32[16,16,16]{1,0,2:T(8,128)S(1)} %select_bitcast_fusion), channel_id=1, replica_groups=mesh['gx'=32,'gy'=16] {'gy'}, use_global_device_ids=true, to_apply=%region_0.1 | all-reduce | flops 4096 | bytes 32768 | tf_op jit(solution)/shard_map/psum | solution.py:89
  (106 shorter events, 52.0 us)
Async XLA Ops:
  0.6 26.6 %copy-start = (f32[16,16,256]{2,1,0:T(8,128)S(1)}, f32[16,16,256]{2,1,0:T(8,128)}, u32[]{:S(2)}) copy-start(f32[16,16,256]{2,1,0:T(8,128)} %param.5) | copy-start | bytes 786436
  1.7 12.2 %collective-permute-start = (f32[16,1,256]{2,1,0:T(1,128)S(1)}, f32[16,1,256]{2,1,0:T(1,128)S(1)}, u32[]{:S(2)}, u32[]{:S(2)}) collective-permute-start(f32[16,1,256]{2,1,0:T(1,128)S(1)} %get-tuple-element.55), channel_id=1, source_target_pairs={{0,16},{16,32},{32,48},{48,64},{64,80},{80,96},{96,112},{112,128},... | collective-permute-start | bytes 49160 | tf_op jit(solution)/shard_map/ppermute | solution.py:20
  3.6 10.3 %collective-permute-start.1 = (f32[16,1,256]{2,1,0:T(1,128)S(1)}, f32[16,1,256]{2,1,0:T(1,128)S(1)}, u32[]{:S(2)}, u32[]{:S(2)}) collective-permute-start(f32[16,1,256]{2,1,0:T(1,128)S(1)} %get-tuple-element.54), channel_id=1, source_target_pairs={{16,0},{32,16},{48,32},{64,48},{80,64},{96,80},{112,96},{128,112},... | collective-permute-start | bytes 49160 | tf_op jit(solution)/shard_map/ppermute | solution.py:21
  8.3 12.0 %collective-permute-start.4 = (f32[16,1,256]{2,1,0:T(1,128)S(1)}, f32[16,1,256]{2,1,0:T(1,128)S(1)}, u32[]{:S(2)}, u32[]{:S(2)}) collective-permute-start(f32[16,1,256]{2,1,0:T(1,128)S(1)} %get-tuple-element.56), channel_id=1, source_target_pairs={{0,16},{16,32},{32,48},{48,64},{64,80},{80,96},{96,112},{112,128},... | collective-permute-start | bytes 49160 | tf_op jit(solution)/shard_map/ppermute | solution.py:20
  10.2 10.1 %collective-permute-start.5 = (f32[16,1,256]{2,1,0:T(1,128)S(1)}, f32[16,1,256]{2,1,0:T(1,128)S(1)}, u32[]{:S(2)}, u32[]{:S(2)}) collective-permute-start(f32[16,1,256]{2,1,0:T(1,128)S(1)} %get-tuple-element.57), channel_id=1, source_target_pairs={{16,0},{32,16},{48,32},{64,48},{80,64},{96,80},{112,96},{128,112},... | collective-permute-start | bytes 49160 | tf_op jit(solution)/shard_map/ppermute | solution.py:21
  15.0 18.3 %copy-start.2 = (f32[16,16,256]{2,1,0:T(8,128)S(1)}, f32[16,16,256]{2,1,0:T(8,128)}, u32[]{:S(2)}) copy-start(f32[16,16,256]{2,1,0:T(8,128)} %param.4) | copy-start | bytes 786436
  15.0 11.3 %collective-permute-start.2 = (f32[16,18,1]{2,1,0:T(8,128)S(1)}, f32[16,18,1]{2,1,0:T(8,128)S(1)}, u32[]{:S(2)}, u32[]{:S(2)}) collective-permute-start(f32[16,18,1]{2,1,0:T(8,128)S(1)} %get-tuple-element.36), channel_id=1, source_target_pairs={{0,1},{1,2},{2,3},{3,4},{4,5},{5,6},{6,7},{7,8},{8,9},{9,10},{10,1... | collective-permute-start | bytes 3464 | tf_op jit(solution)/shard_map/ppermute | solution.py:20
  19.0 8.3 %collective-permute-start.3 = (f32[16,18,1]{2,1,0:T(8,128)S(1)}, f32[16,18,1]{2,1,0:T(8,128)S(1)}, u32[]{:S(2)}, u32[]{:S(2)}) collective-permute-start(f32[16,18,1]{2,1,0:T(8,128)S(1)} %get-tuple-element.37), channel_id=1, source_target_pairs={{1,0},{2,1},{3,2},{4,3},{5,4},{6,5},{7,6},{8,7},{9,8},{10,9},{11,1... | collective-permute-start | bytes 3464 | tf_op jit(solution)/shard_map/ppermute | solution.py:21
  20.5 8.1 %collective-permute-start.6 = (f32[16,18,1]{2,1,0:T(8,128)S(1)}, f32[16,18,1]{2,1,0:T(8,128)S(1)}, u32[]{:S(2)}, u32[]{:S(2)}) collective-permute-start(f32[16,18,1]{2,1,0:T(8,128)S(1)} %get-tuple-element.39), channel_id=1, source_target_pairs={{0,1},{1,2},{2,3},{3,4},{4,5},{5,6},{6,7},{7,8},{8,9},{9,10},{10,1... | collective-permute-start | bytes 3464 | tf_op jit(solution)/shard_map/ppermute | solution.py:20
  25.1 7.9 %collective-permute-start.7 = (f32[16,18,1]{2,1,0:T(8,128)S(1)}, f32[16,18,1]{2,1,0:T(8,128)S(1)}, u32[]{:S(2)}, u32[]{:S(2)}) collective-permute-start(f32[16,18,1]{2,1,0:T(8,128)S(1)} %get-tuple-element.38), channel_id=1, source_target_pairs={{1,0},{2,1},{3,2},{4,3},{5,4},{6,5},{7,6},{8,7},{9,8},{10,9},{11,1... | collective-permute-start | bytes 3464 | tf_op jit(solution)/shard_map/ppermute | solution.py:21
  34.2 5.6 %collective-permute-start.8 = (f32[16,1,256]{2,1,0:T(1,128)S(1)}, f32[16,1,256]{2,1,0:T(1,128)S(1)}, u32[]{:S(2)}, u32[]{:S(2)}) collective-permute-start(f32[16,1,256]{2,1,0:T(1,128)S(1)} %get-tuple-element.52), channel_id=1, source_target_pairs={{0,16},{16,32},{32,48},{48,64},{64,80},{80,96},{96,112},{112,128},... | collective-permute-start | bytes 49160 | tf_op jit(solution)/shard_map/ppermute | solution.py:20
  36.2 5.6 %collective-permute-start.9 = (f32[16,1,256]{2,1,0:T(1,128)S(1)}, f32[16,1,256]{2,1,0:T(1,128)S(1)}, u32[]{:S(2)}, u32[]{:S(2)}) collective-permute-start(f32[16,1,256]{2,1,0:T(1,128)S(1)} %get-tuple-element.53), channel_id=1, source_target_pairs={{16,0},{32,16},{48,32},{64,48},{80,64},{96,80},{112,96},{128,112},... | collective-permute-start | bytes 49160 | tf_op jit(solution)/shard_map/ppermute | solution.py:21
  41.9 8.4 %collective-permute-start.10 = (f32[16,18,1]{2,1,0:T(8,128)S(1)}, f32[16,18,1]{2,1,0:T(8,128)S(1)}, u32[]{:S(2)}, u32[]{:S(2)}) collective-permute-start(f32[16,18,1]{2,1,0:T(8,128)S(1)} %get-tuple-element.35), channel_id=1, source_target_pairs={{0,1},{1,2},{2,3},{3,4},{4,5},{5,6},{6,7},{7,8},{8,9},{9,10},{10,1... | collective-permute-start | bytes 3464 | tf_op jit(solution)/shard_map/ppermute | solution.py:20
  46.6 9.5 %collective-permute-start.11 = (f32[16,18,1]{2,1,0:T(8,128)S(1)}, f32[16,18,1]{2,1,0:T(8,128)S(1)}, u32[]{:S(2)}, u32[]{:S(2)}) collective-permute-start(f32[16,18,1]{2,1,0:T(8,128)S(1)} %get-tuple-element.34), channel_id=1, source_target_pairs={{1,0},{2,1},{3,2},{4,3},{5,4},{6,5},{7,6},{8,7},{9,8},{10,9},{11,1... | collective-permute-start | bytes 3464 | tf_op jit(solution)/shard_map/ppermute | solution.py:21
  57.2 5.6 %collective-permute-start.12 = (f32[16,1,256]{2,1,0:T(1,128)S(1)}, f32[16,1,256]{2,1,0:T(1,128)S(1)}, u32[]{:S(2)}, u32[]{:S(2)}) collective-permute-start(f32[16,1,256]{2,1,0:T(1,128)S(1)} %get-tuple-element.50), channel_id=1, source_target_pairs={{0,16},{16,32},{32,48},{48,64},{64,80},{80,96},{96,112},{112,128},... | collective-permute-start | bytes 49160 | tf_op jit(solution)/shard_map/ppermute | solution.py:20
  60.5 4.1 %collective-permute-start.13 = (f32[16,1,256]{2,1,0:T(1,128)S(1)}, f32[16,1,256]{2,1,0:T(1,128)S(1)}, u32[]{:S(2)}, u32[]{:S(2)}) collective-permute-start(f32[16,1,256]{2,1,0:T(1,128)S(1)} %get-tuple-element.51), channel_id=1, source_target_pairs={{16,0},{32,16},{48,32},{64,48},{80,64},{96,80},{112,96},{128,112},... | collective-permute-start | bytes 49160 | tf_op jit(solution)/shard_map/ppermute | solution.py:21
  64.8 8.3 %collective-permute-start.14 = (f32[16,18,1]{2,1,0:T(8,128)S(1)}, f32[16,18,1]{2,1,0:T(8,128)S(1)}, u32[]{:S(2)}, u32[]{:S(2)}) collective-permute-start(f32[16,18,1]{2,1,0:T(8,128)S(1)} %get-tuple-element.33), channel_id=1, source_target_pairs={{0,1},{1,2},{2,3},{3,4},{4,5},{5,6},{6,7},{7,8},{8,9},{9,10},{10,1... | collective-permute-start | bytes 3464 | tf_op jit(solution)/shard_map/ppermute | solution.py:20
  69.9 7.6 %collective-permute-start.15 = (f32[16,18,1]{2,1,0:T(8,128)S(1)}, f32[16,18,1]{2,1,0:T(8,128)S(1)}, u32[]{:S(2)}, u32[]{:S(2)}) collective-permute-start(f32[16,18,1]{2,1,0:T(8,128)S(1)} %get-tuple-element.32), channel_id=1, source_target_pairs={{1,0},{2,1},{3,2},{4,3},{5,4},{6,5},{7,6},{8,7},{9,8},{10,9},{11,1... | collective-permute-start | bytes 3464 | tf_op jit(solution)/shard_map/ppermute | solution.py:21
  78.5 6.6 %collective-permute-start.16 = (f32[16,1,256]{2,1,0:T(1,128)S(1)}, f32[16,1,256]{2,1,0:T(1,128)S(1)}, u32[]{:S(2)}, u32[]{:S(2)}) collective-permute-start(f32[16,1,256]{2,1,0:T(1,128)S(1)} %get-tuple-element.48), channel_id=1, source_target_pairs={{0,16},{16,32},{32,48},{48,64},{64,80},{80,96},{96,112},{112,128},... | collective-permute-start | bytes 49160 | tf_op jit(solution)/shard_map/ppermute | solution.py:20
  83.2 4.4 %collective-permute-start.17 = (f32[16,1,256]{2,1,0:T(1,128)S(1)}, f32[16,1,256]{2,1,0:T(1,128)S(1)}, u32[]{:S(2)}, u32[]{:S(2)}) collective-permute-start(f32[16,1,256]{2,1,0:T(1,128)S(1)} %get-tuple-element.49), channel_id=1, source_target_pairs={{16,0},{32,16},{48,32},{64,48},{80,64},{96,80},{112,96},{128,112},... | collective-permute-start | bytes 49160 | tf_op jit(solution)/shard_map/ppermute | solution.py:21
  87.8 7.1 %collective-permute-start.18 = (f32[16,18,1]{2,1,0:T(8,128)S(1)}, f32[16,18,1]{2,1,0:T(8,128)S(1)}, u32[]{:S(2)}, u32[]{:S(2)}) collective-permute-start(f32[16,18,1]{2,1,0:T(8,128)S(1)} %get-tuple-element.31), channel_id=1, source_target_pairs={{0,1},{1,2},{2,3},{3,4},{4,5},{5,6},{6,7},{7,8},{8,9},{9,10},{10,1... | collective-permute-start | bytes 3464 | tf_op jit(solution)/shard_map/ppermute | solution.py:20
  91.7 7.6 %collective-permute-start.19 = (f32[16,18,1]{2,1,0:T(8,128)S(1)}, f32[16,18,1]{2,1,0:T(8,128)S(1)}, u32[]{:S(2)}, u32[]{:S(2)}) collective-permute-start(f32[16,18,1]{2,1,0:T(8,128)S(1)} %get-tuple-element.30), channel_id=1, source_target_pairs={{1,0},{2,1},{3,2},{4,3},{5,4},{6,5},{7,6},{8,7},{9,8},{10,9},{11,1... | collective-permute-start | bytes 3464 | tf_op jit(solution)/shard_map/ppermute | solution.py:21
  100.3 6.5 %collective-permute-start.20 = (f32[16,1,256]{2,1,0:T(1,128)S(1)}, f32[16,1,256]{2,1,0:T(1,128)S(1)}, u32[]{:S(2)}, u32[]{:S(2)}) collective-permute-start(f32[16,1,256]{2,1,0:T(1,128)S(1)} %get-tuple-element.46), channel_id=1, source_target_pairs={{0,16},{16,32},{32,48},{48,64},{64,80},{80,96},{96,112},{112,128},... | collective-permute-start | bytes 49160 | tf_op jit(solution)/shard_map/ppermute | solution.py:20
  104.9 4.6 %collective-permute-start.21 = (f32[16,1,256]{2,1,0:T(1,128)S(1)}, f32[16,1,256]{2,1,0:T(1,128)S(1)}, u32[]{:S(2)}, u32[]{:S(2)}) collective-permute-start(f32[16,1,256]{2,1,0:T(1,128)S(1)} %get-tuple-element.47), channel_id=1, source_target_pairs={{16,0},{32,16},{48,32},{64,48},{80,64},{96,80},{112,96},{128,112},... | collective-permute-start | bytes 49160 | tf_op jit(solution)/shard_map/ppermute | solution.py:21
  109.6 7.9 %collective-permute-start.22 = (f32[16,18,1]{2,1,0:T(8,128)S(1)}, f32[16,18,1]{2,1,0:T(8,128)S(1)}, u32[]{:S(2)}, u32[]{:S(2)}) collective-permute-start(f32[16,18,1]{2,1,0:T(8,128)S(1)} %get-tuple-element.29), channel_id=1, source_target_pairs={{0,1},{1,2},{2,3},{3,4},{4,5},{5,6},{6,7},{7,8},{8,9},{9,10},{10,1... | collective-permute-start | bytes 3464 | tf_op jit(solution)/shard_map/ppermute | solution.py:20
  114.4 7.6 %collective-permute-start.23 = (f32[16,18,1]{2,1,0:T(8,128)S(1)}, f32[16,18,1]{2,1,0:T(8,128)S(1)}, u32[]{:S(2)}, u32[]{:S(2)}) collective-permute-start(f32[16,18,1]{2,1,0:T(8,128)S(1)} %get-tuple-element.28), channel_id=1, source_target_pairs={{1,0},{2,1},{3,2},{4,3},{5,4},{6,5},{7,6},{8,7},{9,8},{10,9},{11,1... | collective-permute-start | bytes 3464 | tf_op jit(solution)/shard_map/ppermute | solution.py:21
  122.9 6.9 %collective-permute-start.24 = (f32[16,1,256]{2,1,0:T(1,128)S(1)}, f32[16,1,256]{2,1,0:T(1,128)S(1)}, u32[]{:S(2)}, u32[]{:S(2)}) collective-permute-start(f32[16,1,256]{2,1,0:T(1,128)S(1)} %get-tuple-element.44), channel_id=1, source_target_pairs={{0,16},{16,32},{32,48},{48,64},{64,80},{80,96},{96,112},{112,128},... | collective-permute-start | bytes 49160 | tf_op jit(solution)/shard_map/ppermute | solution.py:20
  127.9 4.2 %collective-permute-start.25 = (f32[16,1,256]{2,1,0:T(1,128)S(1)}, f32[16,1,256]{2,1,0:T(1,128)S(1)}, u32[]{:S(2)}, u32[]{:S(2)}) collective-permute-start(f32[16,1,256]{2,1,0:T(1,128)S(1)} %get-tuple-element.45), channel_id=1, source_target_pairs={{16,0},{32,16},{48,32},{64,48},{80,64},{96,80},{112,96},{128,112},... | collective-permute-start | bytes 49160 | tf_op jit(solution)/shard_map/ppermute | solution.py:21
  132.2 8.3 %collective-permute-start.26 = (f32[16,18,1]{2,1,0:T(8,128)S(1)}, f32[16,18,1]{2,1,0:T(8,128)S(1)}, u32[]{:S(2)}, u32[]{:S(2)}) collective-permute-start(f32[16,18,1]{2,1,0:T(8,128)S(1)} %get-tuple-element.27), channel_id=1, source_target_pairs={{0,1},{1,2},{2,3},{3,4},{4,5},{5,6},{6,7},{7,8},{8,9},{9,10},{10,1... | collective-permute-start | bytes 3464 | tf_op jit(solution)/shard_map/ppermute | solution.py:20
  137.4 7.6 %collective-permute-start.27 = (f32[16,18,1]{2,1,0:T(8,128)S(1)}, f32[16,18,1]{2,1,0:T(8,128)S(1)}, u32[]{:S(2)}, u32[]{:S(2)}) collective-permute-start(f32[16,18,1]{2,1,0:T(8,128)S(1)} %get-tuple-element.26), channel_id=1, source_target_pairs={{1,0},{2,1},{3,2},{4,3},{5,4},{6,5},{7,6},{8,7},{9,8},{10,9},{11,1... | collective-permute-start | bytes 3464 | tf_op jit(solution)/shard_map/ppermute | solution.py:21
  146.0 6.6 %collective-permute-start.28 = (f32[16,1,256]{2,1,0:T(1,128)S(1)}, f32[16,1,256]{2,1,0:T(1,128)S(1)}, u32[]{:S(2)}, u32[]{:S(2)}) collective-permute-start(f32[16,1,256]{2,1,0:T(1,128)S(1)} %get-tuple-element.42), channel_id=1, source_target_pairs={{0,16},{16,32},{32,48},{48,64},{64,80},{80,96},{96,112},{112,128},... | collective-permute-start | bytes 49160 | tf_op jit(solution)/shard_map/ppermute | solution.py:20
  150.6 4.4 %collective-permute-start.29 = (f32[16,1,256]{2,1,0:T(1,128)S(1)}, f32[16,1,256]{2,1,0:T(1,128)S(1)}, u32[]{:S(2)}, u32[]{:S(2)}) collective-permute-start(f32[16,1,256]{2,1,0:T(1,128)S(1)} %get-tuple-element.43), channel_id=1, source_target_pairs={{16,0},{32,16},{48,32},{64,48},{80,64},{96,80},{112,96},{128,112},... | collective-permute-start | bytes 49160 | tf_op jit(solution)/shard_map/ppermute | solution.py:21
  155.3 7.1 %collective-permute-start.30 = (f32[16,18,1]{2,1,0:T(8,128)S(1)}, f32[16,18,1]{2,1,0:T(8,128)S(1)}, u32[]{:S(2)}, u32[]{:S(2)}) collective-permute-start(f32[16,18,1]{2,1,0:T(8,128)S(1)} %get-tuple-element.25), channel_id=1, source_target_pairs={{0,1},{1,2},{2,3},{3,4},{4,5},{5,6},{6,7},{7,8},{8,9},{9,10},{10,1... | collective-permute-start | bytes 3464 | tf_op jit(solution)/shard_map/ppermute | solution.py:20
  159.2 7.6 %collective-permute-start.31 = (f32[16,18,1]{2,1,0:T(8,128)S(1)}, f32[16,18,1]{2,1,0:T(8,128)S(1)}, u32[]{:S(2)}, u32[]{:S(2)}) collective-permute-start(f32[16,18,1]{2,1,0:T(8,128)S(1)} %get-tuple-element.24), channel_id=1, source_target_pairs={{1,0},{2,1},{3,2},{4,3},{5,4},{6,5},{7,6},{8,7},{9,8},{10,9},{11,1... | collective-permute-start | bytes 3464 | tf_op jit(solution)/shard_map/ppermute | solution.py:21
  167.2 15.5 %copy-start.4 = (s32[16,256]{1,0:T(8,128)S(1)}, s32[16,256]{1,0:T(8,128)}, u32[]{:S(2)}) copy-start(s32[16,256]{1,0:T(8,128)} %param.6) | copy-start | bytes 49156
  167.9 21.7 %copy-start.1 = (f32[16,16,256]{2,1,0:T(8,128)}, f32[16,16,256]{2,1,0:T(8,128)S(1)}, u32[]{:S(2)}) copy-start(f32[16,16,256]{2,1,0:T(8,128)S(1)} %fusion.23) | copy-start | bytes 786436
  167.9 6.6 %collective-permute-start.32 = (f32[16,1,256]{2,1,0:T(1,128)S(1)}, f32[16,1,256]{2,1,0:T(1,128)S(1)}, u32[]{:S(2)}, u32[]{:S(2)}) collective-permute-start(f32[16,1,256]{2,1,0:T(1,128)S(1)} %get-tuple-element.40), channel_id=1, source_target_pairs={{0,16},{16,32},{32,48},{48,64},{64,80},{80,96},{96,112},{112,128},... | collective-permute-start | bytes 49160 | tf_op jit(solution)/shard_map/ppermute | solution.py:20
  172.6 4.4 %collective-permute-start.33 = (f32[16,1,256]{2,1,0:T(1,128)S(1)}, f32[16,1,256]{2,1,0:T(1,128)S(1)}, u32[]{:S(2)}, u32[]{:S(2)}) collective-permute-start(f32[16,1,256]{2,1,0:T(1,128)S(1)} %get-tuple-element.41), channel_id=1, source_target_pairs={{16,0},{32,16},{48,32},{64,48},{80,64},{96,80},{112,96},{128,112},... | collective-permute-start | bytes 49160 | tf_op jit(solution)/shard_map/ppermute | solution.py:21
  177.2 7.1 %collective-permute-start.34 = (f32[16,18,1]{2,1,0:T(8,128)S(1)}, f32[16,18,1]{2,1,0:T(8,128)S(1)}, u32[]{:S(2)}, u32[]{:S(2)}) collective-permute-start(f32[16,18,1]{2,1,0:T(8,128)S(1)} %get-tuple-element.23), channel_id=1, source_target_pairs={{0,1},{1,2},{2,3},{3,4},{4,5},{5,6},{6,7},{7,8},{8,9},{9,10},{10,1... | collective-permute-start | bytes 3464 | tf_op jit(solution)/shard_map/ppermute | solution.py:20
  181.2 7.6 %collective-permute-start.35 = (f32[16,18,1]{2,1,0:T(8,128)S(1)}, f32[16,18,1]{2,1,0:T(8,128)S(1)}, u32[]{:S(2)}, u32[]{:S(2)}) collective-permute-start(f32[16,18,1]{2,1,0:T(8,128)S(1)} %get-tuple-element.22), channel_id=1, source_target_pairs={{1,0},{2,1},{3,2},{4,3},{5,4},{6,5},{7,6},{8,7},{9,8},{10,9},{11,1... | collective-permute-start | bytes 3464 | tf_op jit(solution)/shard_map/ppermute | solution.py:21
  189.6 50.4 %copy-start.3 = (f32[16,16,256]{2,1,0:T(8,128)}, f32[16,16,256]{2,1,0:T(8,128)S(1)}, u32[]{:S(2)}) copy-start(f32[16,16,256]{2,1,0:T(8,128)S(1)} %fusion.3) | copy-start | bytes 786436
  189.7 33.9 %copy-start.5 = (s32[16]{0:T(128)S(1)}, s32[16]{0:T(128)}, u32[]{:S(2)}) copy-start(s32[16]{0:T(128)} %param.7) | copy-start | bytes 196
  190.1 5.5 %collective-permute-start.36 = (f32[16,16,256]{2,1,0:T(8,128)S(1)}, f32[16,16,256]{2,1,0:T(8,128)S(1)}, u32[]{:S(2)}, u32[]{:S(2)}) collective-permute-start(f32[16,16,256]{2,1,0:T(8,128)S(1)} %convolution_bitcast_fusion), channel_id=1, source_target_pairs={{0,16},{16,0},{32,48},{48,32},{64,80},{80,64},{96,112},{112,96},{1... | collective-permute-start | bytes 786440 | tf_op jit(solution)/shard_map/ppermute | solution.py:27
  195.7 13.9 %collective-permute-start.37 = (f32[16,16,256]{2,1,0:T(8,128)S(1)}, f32[16,16,256]{2,1,0:T(8,128)S(1)}, u32[]{:S(2)}, u32[]{:S(2)}) collective-permute-start(f32[16,16,256]{2,1,0:T(8,128)S(1)} %select_multiply_fusion.4), channel_id=1, source_target_pairs={{0,32},{16,48},{32,0},{48,16},{64,96},{80,112},{96,64},{112,80},{1... | collective-permute-start | bytes 786440 | tf_op jit(solution)/shard_map/ppermute | solution.py:27
  209.6 11.4 %collective-permute-start.38 = (f32[16,16,256]{2,1,0:T(8,128)S(1)}, f32[16,16,256]{2,1,0:T(8,128)S(1)}, u32[]{:S(2)}, u32[]{:S(2)}) collective-permute-start(f32[16,16,256]{2,1,0:T(8,128)S(1)} %select_multiply_fusion.3), channel_id=1, source_target_pairs={{0,64},{16,80},{32,96},{48,112},{64,0},{80,16},{96,32},{112,48},{1... | collective-permute-start | bytes 786440 | tf_op jit(solution)/shard_map/ppermute | solution.py:27
  221.1 9.0 %collective-permute-start.39 = (f32[16,16,256]{2,1,0:T(8,128)S(1)}, f32[16,16,256]{2,1,0:T(8,128)S(1)}, u32[]{:S(2)}, u32[]{:S(2)}) collective-permute-start(f32[16,16,256]{2,1,0:T(8,128)S(1)} %select_multiply_fusion.2), channel_id=1, source_target_pairs={{0,128},{16,144},{32,160},{48,176},{64,192},{80,208},{96,224},{112... | collective-permute-start | bytes 786440 | tf_op jit(solution)/shard_map/ppermute | solution.py:27
  230.2 9.8 %collective-permute-start.40 = (f32[16,16,256]{2,1,0:T(8,128)S(1)}, f32[16,16,256]{2,1,0:T(8,128)S(1)}, u32[]{:S(2)}, u32[]{:S(2)}) collective-permute-start(f32[16,16,256]{2,1,0:T(8,128)S(1)} %select_multiply_fusion.1), channel_id=1, source_target_pairs={{0,256},{16,272},{32,288},{48,304},{64,320},{80,336},{96,352},{112... | collective-permute-start | bytes 786440 | tf_op jit(solution)/shard_map/ppermute | solution.py:27
where the time goes:
time: 299 us; the launch traced here: 297 us
  starting transfers between devices  127 us (42%)
  waiting for transfers between devices  97.7 us (33%)
  blocking collectives  54.6 us (18%)
  other arithmetic  11.4 us (4%)
  local copies, waits for them, and re-layouts  4.86 us (2%)
    ppermute x18, starting transfers between devices, extended(): before = lax.ppermute(last, axis, up)  72.6 us
    psum x1, blocking collectives, per_device(): sketch = lax.psum(picked, 'gy')  54.6 us
    ppermute x18, waiting for transfers between devices, extended(): after = lax.ppermute(leading, axis, down)  53.5 us
    ppermute x18, starting transfers between devices, extended(): after = lax.ppermute(leading, axis, down)  34.6 us
    ppermute x5, waiting for transfers between devices, partner_2(): lax.ppermute(array, axis, [(i, i ^ 1 << stride) for i in range(lax.axis_s...  29.8 us
    ppermute x5, starting transfers between devices, partner_2(): lax.ppermute(array, axis, [(i, i ^ 1 << stride) for i in range(lax.axis_s...  19.8 us
    ppermute x18, waiting for transfers between devices, extended(): before = lax.ppermute(last, axis, up)  14.4 us
  transfers between devices with their start and end apart: 41, of which 29 were waited for; matrix products, arithmetic and copies ran while one was open for 1% of the time, Pallas kernels for 0%

commit v1 on v0

--- a/solution.py
+++ b/solution.py
@@ -86,7 +86,7 @@
         upper_half = lax.axis_index("gx") >> section_bit & 1 == 1
         current = jnp.where(upper_half, partner - current, current + partner) * half_root
     picked = jnp.take(current, sample_cols, axis=2)
-    sketch = lax.psum(picked, "gy")
+    sketch = jnp.sum(lax.all_gather(picked, "gy"), axis=0)
     return (precond, image_vec, sketch)
 
 

time: 299 us -> 288 us (0.963)
  blocking collectives: 54.6 us -> 43.2 us
    psum x1 -> x0, blocking collectives: 54.6 us -> none  [per_device(): sketch = lax.psum(picked, 'gy')]
    all_gather x0 -> x1, blocking collectives: none -> 43.2 us  [per_device(): sketch = jnp.sum(lax.all_gather(picked, 'gy'), axis=0)]
where the time goes in v1:
time: 288 us; the launch traced here: 286 us
  starting transfers between devices  127 us (44%)
  waiting for transfers between devices  97.7 us (34%)
  blocking collectives  43.2 us (15%)
  other arithmetic  12.2 us (4%)
  local copies, waits for them, and re-layouts  4.2 us (1%)
    ppermute x18, starting transfers between devices, extended(): before = lax.ppermute(last, axis, up)  72.6 us
    ppermute x18, waiting for transfers between devices, extended(): after = lax.ppermute(leading, axis, down)  53.5 us
    all_gather x1, blocking collectives, per_device(): sketch = jnp.sum(lax.all_gather(picked, 'gy'), axis=0)  43.2 us
    ppermute x18, starting transfers between devices, extended(): after = lax.ppermute(leading, axis, down)  34.6 us
    ppermute x5, waiting for transfers between devices, partner_2(): lax.ppermute(array, axis, [(i, i ^ 1 << stride) for i in range(lax.axis_s...  29.8 us
    ppermute x5, starting transfers between devices, partner_2(): lax.ppermute(array, axis, [(i, i ^ 1 << stride) for i in range(lax.axis_s...  19.8 us
    ppermute x18, waiting for transfers between devices, extended(): before = lax.ppermute(last, axis, up)  14.4 us
  transfers between devices with their start and end apart: 41, of which 29 were waited for; matrix products, arithmetic and copies ran while one was open for 1% of the time, Pallas kernels for 0%

profile of v1, /device:TPU:18, one launch (start us, length us, event | category | flops | bytes accessed | tf_op | source)
XLA Modules:
  0.0 286.1 jit_solution(508327244619370837)
XLA Ops:
  1.7 1.9 collective-permute-start
  3.6 3.6 %collective-permute-start.1 = (f32[16,1,256]{2,1,0:T(1,128)S(1)}, f32[16,1,256]{2,1,0:T(1,128)S(1)}, u32[]{:S(2)}, u32[]{:S(2)}) collective-permute-start(f32[16,1,256]{2,1,0:T(1,128)S(1)} %get-tuple-element.54), channel_id=1, source_target_pairs={{16,0},{32,16},{48,32},{64,48},{80,64},{96,80},{112,96},{128,112},... | collective-permute-start | bytes 49160 | tf_op jit(solution)/shard_map/ppermute | solution.py:21
  8.3 1.9 collective-permute-start.4
  10.2 3.6 %collective-permute-start.5 = (f32[16,1,256]{2,1,0:T(1,128)S(1)}, f32[16,1,256]{2,1,0:T(1,128)S(1)}, u32[]{:S(2)}, u32[]{:S(2)}) collective-permute-start(f32[16,1,256]{2,1,0:T(1,128)S(1)} %get-tuple-element.57), channel_id=1, source_target_pairs={{16,0},{32,16},{48,32},{64,48},{80,64},{96,80},{112,96},{128,112},... | collective-permute-start | bytes 49160 | tf_op jit(solution)/shard_map/ppermute | solution.py:21
  15.0 4.0 %collective-permute-start.2 = (f32[16,18,1]{2,1,0:T(8,128)S(1)}, f32[16,18,1]{2,1,0:T(8,128)S(1)}, u32[]{:S(2)}, u32[]{:S(2)}) collective-permute-start(f32[16,18,1]{2,1,0:T(8,128)S(1)} %get-tuple-element.36), channel_id=1, source_target_pairs={{0,1},{1,2},{2,3},{3,4},{4,5},{5,6},{6,7},{7,8},{8,9},{9,10},{10,1... | collective-permute-start | bytes 3464 | tf_op jit(solution)/shard_map/ppermute | solution.py:20
  20.5 4.6 %collective-permute-start.6 = (f32[16,18,1]{2,1,0:T(8,128)S(1)}, f32[16,18,1]{2,1,0:T(8,128)S(1)}, u32[]{:S(2)}, u32[]{:S(2)}) collective-permute-start(f32[16,18,1]{2,1,0:T(8,128)S(1)} %get-tuple-element.39), channel_id=1, source_target_pairs={{0,1},{1,2},{2,3},{3,4},{4,5},{5,6},{6,7},{7,8},{8,9},{9,10},{10,1... | collective-permute-start | bytes 3464 | tf_op jit(solution)/shard_map/ppermute | solution.py:20
  28.6 4.3 %collective-permute-done.7 = f32[16,18,1]{2,1,0:T(8,128)S(1)} collective-permute-done((f32[16,18,1]{2,1,0:T(8,128)S(1)}, f32[16,18,1]{2,1,0:T(8,128)S(1)}, u32[]{:S(2)}, u32[]{:S(2)}) %collective-permute-start.7) | collective-permute-done | bytes 1184 | tf_op jit(solution)/shard_map/ppermute | solution.py:21
  34.2 1.9 collective-permute-start.8
  36.2 3.6 %collective-permute-start.9 = (f32[16,1,256]{2,1,0:T(1,128)S(1)}, f32[16,1,256]{2,1,0:T(1,128)S(1)}, u32[]{:S(2)}, u32[]{:S(2)}) collective-permute-start(f32[16,1,256]{2,1,0:T(1,128)S(1)} %get-tuple-element.53), channel_id=1, source_target_pairs={{16,0},{32,16},{48,32},{64,48},{80,64},{96,80},{112,96},{128,112},... | collective-permute-start | bytes 49160 | tf_op jit(solution)/shard_map/ppermute | solution.py:21
  41.9 4.7 %collective-permute-start.10 = (f32[16,18,1]{2,1,0:T(8,128)S(1)}, f32[16,18,1]{2,1,0:T(8,128)S(1)}, u32[]{:S(2)}, u32[]{:S(2)}) collective-permute-start(f32[16,18,1]{2,1,0:T(8,128)S(1)} %get-tuple-element.35), channel_id=1, source_target_pairs={{0,1},{1,2},{2,3},{3,4},{4,5},{5,6},{6,7},{7,8},{8,9},{9,10},{10,1... | collective-permute-start | bytes 3464 | tf_op jit(solution)/shard_map/ppermute | solution.py:20
  47.9 2.4 collective-permute-done.10
  50.3 5.8 %collective-permute-done.11 = f32[16,18,1]{2,1,0:T(8,128)S(1)} collective-permute-done((f32[16,18,1]{2,1,0:T(8,128)S(1)}, f32[16,18,1]{2,1,0:T(8,128)S(1)}, u32[]{:S(2)}, u32[]{:S(2)}) %collective-permute-start.11) | collective-permute-done | bytes 1184 | tf_op jit(solution)/shard_map/ppermute | solution.py:21
  57.2 3.3 %collective-permute-start.12 = (f32[16,1,256]{2,1,0:T(1,128)S(1)}, f32[16,1,256]{2,1,0:T(1,128)S(1)}, u32[]{:S(2)}, u32[]{:S(2)}) collective-permute-start(f32[16,1,256]{2,1,0:T(1,128)S(1)} %get-tuple-element.50), channel_id=1, source_target_pairs={{0,16},{16,32},{32,48},{48,64},{64,80},{80,96},{96,112},{112,128},... | collective-permute-start | bytes 49160 | tf_op jit(solution)/shard_map/ppermute | solution.py:20
  60.5 2.3 collective-permute-start.13
  64.8 5.1 %collective-permute-start.14 = (f32[16,18,1]{2,1,0:T(8,128)S(1)}, f32[16,18,1]{2,1,0:T(8,128)S(1)}, u32[]{:S(2)}, u32[]{:S(2)}) collective-permute-start(f32[16,18,1]{2,1,0:T(8,128)S(1)} %get-tuple-element.33), channel_id=1, source_target_pairs={{0,1},{1,2},{2,3},{3,4},{4,5},{5,6},{6,7},{7,8},{8,9},{9,10},{10,1... | collective-permute-start | bytes 3464 | tf_op jit(solution)/shard_map/ppermute | solution.py:20
  73.1 4.4 %collective-permute-done.15 = f32[16,18,1]{2,1,0:T(8,128)S(1)} collective-permute-done((f32[16,18,1]{2,1,0:T(8,128)S(1)}, f32[16,18,1]{2,1,0:T(8,128)S(1)}, u32[]{:S(2)}, u32[]{:S(2)}) %collective-permute-start.15) | collective-permute-done | bytes 1184 | tf_op jit(solution)/shard_map/ppermute | solution.py:21
  78.5 4.7 %collective-permute-start.16 = (f32[16,1,256]{2,1,0:T(1,128)S(1)}, f32[16,1,256]{2,1,0:T(1,128)S(1)}, u32[]{:S(2)}, u32[]{:S(2)}) collective-permute-start(f32[16,1,256]{2,1,0:T(1,128)S(1)} %get-tuple-element.48), channel_id=1, source_target_pairs={{0,16},{16,32},{32,48},{48,64},{64,80},{80,96},{96,112},{112,128},... | collective-permute-start | bytes 49160 | tf_op jit(solution)/shard_map/ppermute | solution.py:20
  83.2 1.9 collective-permute-start.17
  85.1 2.5 collective-permute-done.17
  87.8 3.9 %collective-permute-start.18 = (f32[16,18,1]{2,1,0:T(8,128)S(1)}, f32[16,18,1]{2,1,0:T(8,128)S(1)}, u32[]{:S(2)}, u32[]{:S(2)}) collective-permute-start(f32[16,18,1]{2,1,0:T(8,128)S(1)} %get-tuple-element.31), channel_id=1, source_target_pairs={{0,1},{1,2},{2,3},{3,4},{4,5},{5,6},{6,7},{7,8},{8,9},{9,10},{10,1... | collective-permute-start | bytes 3464 | tf_op jit(solution)/shard_map/ppermute | solution.py:20
  94.9 4.4 %collective-permute-done.19 = f32[16,18,1]{2,1,0:T(8,128)S(1)} collective-permute-done((f32[16,18,1]{2,1,0:T(8,128)S(1)}, f32[16,18,1]{2,1,0:T(8,128)S(1)}, u32[]{:S(2)}, u32[]{:S(2)}) %collective-permute-start.19) | collective-permute-done | bytes 1184 | tf_op jit(solution)/shard_map/ppermute | solution.py:21
  100.3 4.5 %collective-permute-start.20 = (f32[16,1,256]{2,1,0:T(1,128)S(1)}, f32[16,1,256]{2,1,0:T(1,128)S(1)}, u32[]{:S(2)}, u32[]{:S(2)}) collective-permute-start(f32[16,1,256]{2,1,0:T(1,128)S(1)} %get-tuple-element.46), channel_id=1, source_target_pairs={{0,16},{16,32},{32,48},{48,64},{64,80},{80,96},{96,112},{112,128},... | collective-permute-start | bytes 49160 | tf_op jit(solution)/shard_map/ppermute | solution.py:20
  104.9 1.9 collective-permute-start.21
  106.8 2.6 collective-permute-done.21
  109.6 4.7 %collective-permute-start.22 = (f32[16,18,1]{2,1,0:T(8,128)S(1)}, f32[16,18,1]{2,1,0:T(8,128)S(1)}, u32[]{:S(2)}, u32[]{:S(2)}) collective-permute-start(f32[16,18,1]{2,1,0:T(8,128)S(1)} %get-tuple-element.29), channel_id=1, source_target_pairs={{0,1},{1,2},{2,3},{3,4},{4,5},{5,6},{6,7},{7,8},{8,9},{9,10},{10,1... | collective-permute-start | bytes 3464 | tf_op jit(solution)/shard_map/ppermute | solution.py:20
  117.5 4.4 %collective-permute-done.23 = f32[16,18,1]{2,1,0:T(8,128)S(1)} collective-permute-done((f32[16,18,1]{2,1,0:T(8,128)S(1)}, f32[16,18,1]{2,1,0:T(8,128)S(1)}, u32[]{:S(2)}, u32[]{:S(2)}) %collective-permute-start.23) | collective-permute-done | bytes 1184 | tf_op jit(solution)/shard_map/ppermute | solution.py:21
  122.9 4.9 %collective-permute-start.24 = (f32[16,1,256]{2,1,0:T(1,128)S(1)}, f32[16,1,256]{2,1,0:T(1,128)S(1)}, u32[]{:S(2)}, u32[]{:S(2)}) collective-permute-start(f32[16,1,256]{2,1,0:T(1,128)S(1)} %get-tuple-element.44), channel_id=1, source_target_pairs={{0,16},{16,32},{32,48},{48,64},{64,80},{80,96},{96,112},{112,128},... | collective-permute-start | bytes 49160 | tf_op jit(solution)/shard_map/ppermute | solution.py:20
  129.8 2.2 collective-permute-done.25
  132.2 5.1 %collective-permute-start.26 = (f32[16,18,1]{2,1,0:T(8,128)S(1)}, f32[16,18,1]{2,1,0:T(8,128)S(1)}, u32[]{:S(2)}, u32[]{:S(2)}) collective-permute-start(f32[16,18,1]{2,1,0:T(8,128)S(1)} %get-tuple-element.27), channel_id=1, source_target_pairs={{0,1},{1,2},{2,3},{3,4},{4,5},{5,6},{6,7},{7,8},{8,9},{9,10},{10,1... | collective-permute-start | bytes 3464 | tf_op jit(solution)/shard_map/ppermute | solution.py:20
  140.5 4.4 %collective-permute-done.27 = f32[16,18,1]{2,1,0:T(8,128)S(1)} collective-permute-done((f32[16,18,1]{2,1,0:T(8,128)S(1)}, f32[16,18,1]{2,1,0:T(8,128)S(1)}, u32[]{:S(2)}, u32[]{:S(2)}) %collective-permute-start.27) | collective-permute-done | bytes 1184 | tf_op jit(solution)/shard_map/ppermute | solution.py:21
  146.0 4.7 %collective-permute-start.28 = (f32[16,1,256]{2,1,0:T(1,128)S(1)}, f32[16,1,256]{2,1,0:T(1,128)S(1)}, u32[]{:S(2)}, u32[]{:S(2)}) collective-permute-start(f32[16,1,256]{2,1,0:T(1,128)S(1)} %get-tuple-element.42), channel_id=1, source_target_pairs={{0,16},{16,32},{32,48},{48,64},{64,80},{80,96},{96,112},{112,128},... | collective-permute-start | bytes 49160 | tf_op jit(solution)/shard_map/ppermute | solution.py:20
  152.6 2.5 collective-permute-done.29
  155.3 3.9 %collective-permute-start.30 = (f32[16,18,1]{2,1,0:T(8,128)S(1)}, f32[16,18,1]{2,1,0:T(8,128)S(1)}, u32[]{:S(2)}, u32[]{:S(2)}) collective-permute-start(f32[16,18,1]{2,1,0:T(8,128)S(1)} %get-tuple-element.25), channel_id=1, source_target_pairs={{0,1},{1,2},{2,3},{3,4},{4,5},{5,6},{6,7},{7,8},{8,9},{9,10},{10,1... | collective-permute-start | bytes 3464 | tf_op jit(solution)/shard_map/ppermute | solution.py:20
  162.4 4.4 %collective-permute-done.31 = f32[16,18,1]{2,1,0:T(8,128)S(1)} collective-permute-done((f32[16,18,1]{2,1,0:T(8,128)S(1)}, f32[16,18,1]{2,1,0:T(8,128)S(1)}, u32[]{:S(2)}, u32[]{:S(2)}) %collective-permute-start.31) | collective-permute-done | bytes 1184 | tf_op jit(solution)/shard_map/ppermute | solution.py:21
  167.9 4.7 %collective-permute-start.32 = (f32[16,1,256]{2,1,0:T(1,128)S(1)}, f32[16,1,256]{2,1,0:T(1,128)S(1)}, u32[]{:S(2)}, u32[]{:S(2)}) collective-permute-start(f32[16,1,256]{2,1,0:T(1,128)S(1)} %get-tuple-element.40), channel_id=1, source_target_pairs={{0,16},{16,32},{32,48},{48,64},{64,80},{80,96},{96,112},{112,128},... | collective-permute-start | bytes 49160 | tf_op jit(solution)/shard_map/ppermute | solution.py:20
  174.5 2.5 collective-permute-done.33
  177.2 3.9 %collective-permute-start.34 = (f32[16,18,1]{2,1,0:T(8,128)S(1)}, f32[16,18,1]{2,1,0:T(8,128)S(1)}, u32[]{:S(2)}, u32[]{:S(2)}) collective-permute-start(f32[16,18,1]{2,1,0:T(8,128)S(1)} %get-tuple-element.23), channel_id=1, source_target_pairs={{0,1},{1,2},{2,3},{3,4},{4,5},{5,6},{6,7},{7,8},{8,9},{9,10},{10,1... | collective-permute-start | bytes 3464 | tf_op jit(solution)/shard_map/ppermute | solution.py:20
  184.3 4.4 %collective-permute-done.35 = f32[16,18,1]{2,1,0:T(8,128)S(1)} collective-permute-done((f32[16,18,1]{2,1,0:T(8,128)S(1)}, f32[16,18,1]{2,1,0:T(8,128)S(1)}, u32[]{:S(2)}, u32[]{:S(2)}) %collective-permute-start.35) | collective-permute-done | bytes 1184 | tf_op jit(solution)/shard_map/ppermute | solution.py:21
  190.1 4.4 %collective-permute-start.36 = (f32[16,16,256]{2,1,0:T(8,128)S(1)}, f32[16,16,256]{2,1,0:T(8,128)S(1)}, u32[]{:S(2)}, u32[]{:S(2)}) collective-permute-start(f32[16,16,256]{2,1,0:T(8,128)S(1)} %convolution_bitcast_fusion), channel_id=1, source_target_pairs={{0,16},{16,0},{32,48},{48,32},{64,80},{80,64},{96,112},{112,96},{1... | collective-permute-start | bytes 786440 | tf_op jit(solution)/shard_map/ppermute | solution.py:27
  195.7 7.1 %collective-permute-start.37 = (f32[16,16,256]{2,1,0:T(8,128)S(1)}, f32[16,16,256]{2,1,0:T(8,128)S(1)}, u32[]{:S(2)}, u32[]{:S(2)}) collective-permute-start(f32[16,16,256]{2,1,0:T(8,128)S(1)} %select_multiply_fusion.4), channel_id=1, source_target_pairs={{0,32},{16,48},{32,0},{48,16},{64,96},{80,112},{96,64},{112,80},{1... | collective-permute-start | bytes 786440 | tf_op jit(solution)/shard_map/ppermute | solution.py:27
  202.8 6.8 %collective-permute-done.37 = f32[16,16,256]{2,1,0:T(8,128)S(1)} collective-permute-done((f32[16,16,256]{2,1,0:T(8,128)S(1)}, f32[16,16,256]{2,1,0:T(8,128)S(1)}, u32[]{:S(2)}, u32[]{:S(2)}) %collective-permute-start.37) | collective-permute-done | bytes 262176 | tf_op jit(solution)/shard_map/ppermute | solution.py:27
  209.6 3.0 %collective-permute-start.38 = (f32[16,16,256]{2,1,0:T(8,128)S(1)}, f32[16,16,256]{2,1,0:T(8,128)S(1)}, u32[]{:S(2)}, u32[]{:S(2)}) collective-permute-start(f32[16,16,256]{2,1,0:T(8,128)S(1)} %select_multiply_fusion.3), channel_id=1, source_target_pairs={{0,64},{16,80},{32,96},{48,112},{64,0},{80,16},{96,32},{112,48},{1... | collective-permute-start | bytes 786440 | tf_op jit(solution)/shard_map/ppermute | solution.py:27
  212.7 8.4 %collective-permute-done.38 = f32[16,16,256]{2,1,0:T(8,128)S(1)} collective-permute-done((f32[16,16,256]{2,1,0:T(8,128)S(1)}, f32[16,16,256]{2,1,0:T(8,128)S(1)}, u32[]{:S(2)}, u32[]{:S(2)}) %collective-permute-start.38) | collective-permute-done | bytes 262176 | tf_op jit(solution)/shard_map/ppermute | solution.py:27
  221.1 2.4 collective-permute-start.39
  223.6 6.5 %collective-permute-done.39 = f32[16,16,256]{2,1,0:T(8,128)S(1)} collective-permute-done((f32[16,16,256]{2,1,0:T(8,128)S(1)}, f32[16,16,256]{2,1,0:T(8,128)S(1)}, u32[]{:S(2)}, u32[]{:S(2)}) %collective-permute-start.39) | collective-permute-done | bytes 262176 | tf_op jit(solution)/shard_map/ppermute | solution.py:27
  230.2 2.8 collective-permute-start.40
  233.1 6.9 %collective-permute-done.40 = f32[16,16,256]{2,1,0:T(8,128)S(1)} collective-permute-done((f32[16,16,256]{2,1,0:T(8,128)S(1)}, f32[16,16,256]{2,1,0:T(8,128)S(1)}, u32[]{:S(2)}, u32[]{:S(2)}) %collective-permute-start.40) | collective-permute-done | bytes 262176 | tf_op jit(solution)/shard_map/ppermute | solution.py:27
  242.1 43.2 %all_gather.4 = f32[16,16,16,16]{3,2,1,0:T(8,128)S(1)} all-gather(f32[1,16,16,16]{3,2,1,0:T(8,128)S(1)} %copy.9), channel_id=1, replica_groups=mesh['gx'=32,'gy'=16] {'gy'}, dimensions={0}, use_global_device_ids=true | all-gather | bytes 278528 | tf_op jit(solution)/shard_map/all_gather | solution.py:89
  (107 shorter events, 52.1 us)
Async XLA Ops:
  0.6 26.6 %copy-start = (f32[16,16,256]{2,1,0:T(8,128)S(1)}, f32[16,16,256]{2,1,0:T(8,128)}, u32[]{:S(2)}) copy-start(f32[16,16,256]{2,1,0:T(8,128)} %param.5) | copy-start | bytes 786436
  1.7 12.2 %collective-permute-start = (f32[16,1,256]{2,1,0:T(1,128)S(1)}, f32[16,1,256]{2,1,0:T(1,128)S(1)}, u32[]{:S(2)}, u32[]{:S(2)}) collective-permute-start(f32[16,1,256]{2,1,0:T(1,128)S(1)} %get-tuple-element.55), channel_id=1, source_target_pairs={{0,16},{16,32},{32,48},{48,64},{64,80},{80,96},{96,112},{112,128},... | collective-permute-start | bytes 49160 | tf_op jit(solution)/shard_map/ppermute | solution.py:20
  3.6 10.3 %collective-permute-start.1 = (f32[16,1,256]{2,1,0:T(1,128)S(1)}, f32[16,1,256]{2,1,0:T(1,128)S(1)}, u32[]{:S(2)}, u32[]{:S(2)}) collective-permute-start(f32[16,1,256]{2,1,0:T(1,128)S(1)} %get-tuple-element.54), channel_id=1, source_target_pairs={{16,0},{32,16},{48,32},{64,48},{80,64},{96,80},{112,96},{128,112},... | collective-permute-start | bytes 49160 | tf_op jit(solution)/shard_map/ppermute | solution.py:21
  8.3 12.0 %collective-permute-start.4 = (f32[16,1,256]{2,1,0:T(1,128)S(1)}, f32[16,1,256]{2,1,0:T(1,128)S(1)}, u32[]{:S(2)}, u32[]{:S(2)}) collective-permute-start(f32[16,1,256]{2,1,0:T(1,128)S(1)} %get-tuple-element.56), channel_id=1, source_target_pairs={{0,16},{16,32},{32,48},{48,64},{64,80},{80,96},{96,112},{112,128},... | collective-permute-start | bytes 49160 | tf_op jit(solution)/shard_map/ppermute | solution.py:20
  10.2 10.1 %collective-permute-start.5 = (f32[16,1,256]{2,1,0:T(1,128)S(1)}, f32[16,1,256]{2,1,0:T(1,128)S(1)}, u32[]{:S(2)}, u32[]{:S(2)}) collective-permute-start(f32[16,1,256]{2,1,0:T(1,128)S(1)} %get-tuple-element.57), channel_id=1, source_target_pairs={{16,0},{32,16},{48,32},{64,48},{80,64},{96,80},{112,96},{128,112},... | collective-permute-start | bytes 49160 | tf_op jit(solution)/shard_map/ppermute | solution.py:21
  15.0 18.3 %copy-start.2 = (f32[16,16,256]{2,1,0:T(8,128)S(1)}, f32[16,16,256]{2,1,0:T(8,128)}, u32[]{:S(2)}) copy-start(f32[16,16,256]{2,1,0:T(8,128)} %param.4) | copy-start | bytes 786436
  15.0 11.3 %collective-permute-start.2 = (f32[16,18,1]{2,1,0:T(8,128)S(1)}, f32[16,18,1]{2,1,0:T(8,128)S(1)}, u32[]{:S(2)}, u32[]{:S(2)}) collective-permute-start(f32[16,18,1]{2,1,0:T(8,128)S(1)} %get-tuple-element.36), channel_id=1, source_target_pairs={{0,1},{1,2},{2,3},{3,4},{4,5},{5,6},{6,7},{7,8},{8,9},{9,10},{10,1... | collective-permute-start | bytes 3464 | tf_op jit(solution)/shard_map/ppermute | solution.py:20
  19.0 8.3 %collective-permute-start.3 = (f32[16,18,1]{2,1,0:T(8,128)S(1)}, f32[16,18,1]{2,1,0:T(8,128)S(1)}, u32[]{:S(2)}, u32[]{:S(2)}) collective-permute-start(f32[16,18,1]{2,1,0:T(8,128)S(1)} %get-tuple-element.37), channel_id=1, source_target_pairs={{1,0},{2,1},{3,2},{4,3},{5,4},{6,5},{7,6},{8,7},{9,8},{10,9},{11,1... | collective-permute-start | bytes 3464 | tf_op jit(solution)/shard_map/ppermute | solution.py:21
  20.5 8.1 %collective-permute-start.6 = (f32[16,18,1]{2,1,0:T(8,128)S(1)}, f32[16,18,1]{2,1,0:T(8,128)S(1)}, u32[]{:S(2)}, u32[]{:S(2)}) collective-permute-start(f32[16,18,1]{2,1,0:T(8,128)S(1)} %get-tuple-element.39), channel_id=1, source_target_pairs={{0,1},{1,2},{2,3},{3,4},{4,5},{5,6},{6,7},{7,8},{8,9},{9,10},{10,1... | collective-permute-start | bytes 3464 | tf_op jit(solution)/shard_map/ppermute | solution.py:20
  25.1 7.9 %collective-permute-start.7 = (f32[16,18,1]{2,1,0:T(8,128)S(1)}, f32[16,18,1]{2,1,0:T(8,128)S(1)}, u32[]{:S(2)}, u32[]{:S(2)}) collective-permute-start(f32[16,18,1]{2,1,0:T(8,128)S(1)} %get-tuple-element.38), channel_id=1, source_target_pairs={{1,0},{2,1},{3,2},{4,3},{5,4},{6,5},{7,6},{8,7},{9,8},{10,9},{11,1... | collective-permute-start | bytes 3464 | tf_op jit(solution)/shard_map/ppermute | solution.py:21
  34.2 5.6 %collective-permute-start.8 = (f32[16,1,256]{2,1,0:T(1,128)S(1)}, f32[16,1,256]{2,1,0:T(1,128)S(1)}, u32[]{:S(2)}, u32[]{:S(2)}) collective-permute-start(f32[16,1,256]{2,1,0:T(1,128)S(1)} %get-tuple-element.52), channel_id=1, source_target_pairs={{0,16},{16,32},{32,48},{48,64},{64,80},{80,96},{96,112},{112,128},... | collective-permute-start | bytes 49160 | tf_op jit(solution)/shard_map/ppermute | solution.py:20
  36.2 5.6 %collective-permute-start.9 = (f32[16,1,256]{2,1,0:T(1,128)S(1)}, f32[16,1,256]{2,1,0:T(1,128)S(1)}, u32[]{:S(2)}, u32[]{:S(2)}) collective-permute-start(f32[16,1,256]{2,1,0:T(1,128)S(1)} %get-tuple-element.53), channel_id=1, source_target_pairs={{16,0},{32,16},{48,32},{64,48},{80,64},{96,80},{112,96},{128,112},... | collective-permute-start | bytes 49160 | tf_op jit(solution)/shard_map/ppermute | solution.py:21
  41.9 8.4 %collective-permute-start.10 = (f32[16,18,1]{2,1,0:T(8,128)S(1)}, f32[16,18,1]{2,1,0:T(8,128)S(1)}, u32[]{:S(2)}, u32[]{:S(2)}) collective-permute-start(f32[16,18,1]{2,1,0:T(8,128)S(1)} %get-tuple-element.35), channel_id=1, source_target_pairs={{0,1},{1,2},{2,3},{3,4},{4,5},{5,6},{6,7},{7,8},{8,9},{9,10},{10,1... | collective-permute-start | bytes 3464 | tf_op jit(solution)/shard_map/ppermute | solution.py:20
  46.6 9.5 %collective-permute-start.11 = (f32[16,18,1]{2,1,0:T(8,128)S(1)}, f32[16,18,1]{2,1,0:T(8,128)S(1)}, u32[]{:S(2)}, u32[]{:S(2)}) collective-permute-start(f32[16,18,1]{2,1,0:T(8,128)S(1)} %get-tuple-element.34), channel_id=1, source_target_pairs={{1,0},{2,1},{3,2},{4,3},{5,4},{6,5},{7,6},{8,7},{9,8},{10,9},{11,1... | collective-permute-start | bytes 3464 | tf_op jit(solution)/shard_map/ppermute | solution.py:21
  57.2 5.6 %collective-permute-start.12 = (f32[16,1,256]{2,1,0:T(1,128)S(1)}, f32[16,1,256]{2,1,0:T(1,128)S(1)}, u32[]{:S(2)}, u32[]{:S(2)}) collective-permute-start(f32[16,1,256]{2,1,0:T(1,128)S(1)} %get-tuple-element.50), channel_id=1, source_target_pairs={{0,16},{16,32},{32,48},{48,64},{64,80},{80,96},{96,112},{112,128},... | collective-permute-start | bytes 49160 | tf_op jit(solution)/shard_map/ppermute | solution.py:20
  60.5 4.1 %collective-permute-start.13 = (f32[16,1,256]{2,1,0:T(1,128)S(1)}, f32[16,1,256]{2,1,0:T(1,128)S(1)}, u32[]{:S(2)}, u32[]{:S(2)}) collective-permute-start(f32[16,1,256]{2,1,0:T(1,128)S(1)} %get-tuple-element.51), channel_id=1, source_target_pairs={{16,0},{32,16},{48,32},{64,48},{80,64},{96,80},{112,96},{128,112},... | collective-permute-start | bytes 49160 | tf_op jit(solution)/shard_map/ppermute | solution.py:21
  64.8 8.3 %collective-permute-start.14 = (f32[16,18,1]{2,1,0:T(8,128)S(1)}, f32[16,18,1]{2,1,0:T(8,128)S(1)}, u32[]{:S(2)}, u32[]{:S(2)}) collective-permute-start(f32[16,18,1]{2,1,0:T(8,128)S(1)} %get-tuple-element.33), channel_id=1, source_target_pairs={{0,1},{1,2},{2,3},{3,4},{4,5},{5,6},{6,7},{7,8},{8,9},{9,10},{10,1... | collective-permute-start | bytes 3464 | tf_op jit(solution)/shard_map/ppermute | solution.py:20
  69.9 7.6 %collective-permute-start.15 = (f32[16,18,1]{2,1,0:T(8,128)S(1)}, f32[16,18,1]{2,1,0:T(8,128)S(1)}, u32[]{:S(2)}, u32[]{:S(2)}) collective-permute-start(f32[16,18,1]{2,1,0:T(8,128)S(1)} %get-tuple-element.32), channel_id=1, source_target_pairs={{1,0},{2,1},{3,2},{4,3},{5,4},{6,5},{7,6},{8,7},{9,8},{10,9},{11,1... | collective-permute-start | bytes 3464 | tf_op jit(solution)/shard_map/ppermute | solution.py:21
  78.5 6.6 %collective-permute-start.16 = (f32[16,1,256]{2,1,0:T(1,128)S(1)}, f32[16,1,256]{2,1,0:T(1,128)S(1)}, u32[]{:S(2)}, u32[]{:S(2)}) collective-permute-start(f32[16,1,256]{2,1,0:T(1,128)S(1)} %get-tuple-element.48), channel_id=1, source_target_pairs={{0,16},{16,32},{32,48},{48,64},{64,80},{80,96},{96,112},{112,128},... | collective-permute-start | bytes 49160 | tf_op jit(solution)/shard_map/ppermute | solution.py:20
  83.2 4.4 %collective-permute-start.17 = (f32[16,1,256]{2,1,0:T(1,128)S(1)}, f32[16,1,256]{2,1,0:T(1,128)S(1)}, u32[]{:S(2)}, u32[]{:S(2)}) collective-permute-start(f32[16,1,256]{2,1,0:T(1,128)S(1)} %get-tuple-element.49), channel_id=1, source_target_pairs={{16,0},{32,16},{48,32},{64,48},{80,64},{96,80},{112,96},{128,112},... | collective-permute-start | bytes 49160 | tf_op jit(solution)/shard_map/ppermute | solution.py:21
  87.8 7.1 %collective-permute-start.18 = (f32[16,18,1]{2,1,0:T(8,128)S(1)}, f32[16,18,1]{2,1,0:T(8,128)S(1)}, u32[]{:S(2)}, u32[]{:S(2)}) collective-permute-start(f32[16,18,1]{2,1,0:T(8,128)S(1)} %get-tuple-element.31), channel_id=1, source_target_pairs={{0,1},{1,2},{2,3},{3,4},{4,5},{5,6},{6,7},{7,8},{8,9},{9,10},{10,1... | collective-permute-start | bytes 3464 | tf_op jit(solution)/shard_map/ppermute | solution.py:20
  91.7 7.6 %collective-permute-start.19 = (f32[16,18,1]{2,1,0:T(8,128)S(1)}, f32[16,18,1]{2,1,0:T(8,128)S(1)}, u32[]{:S(2)}, u32[]{:S(2)}) collective-permute-start(f32[16,18,1]{2,1,0:T(8,128)S(1)} %get-tuple-element.30), channel_id=1, source_target_pairs={{1,0},{2,1},{3,2},{4,3},{5,4},{6,5},{7,6},{8,7},{9,8},{10,9},{11,1... | collective-permute-start | bytes 3464 | tf_op jit(solution)/shard_map/ppermute | solution.py:21
  100.3 6.5 %collective-permute-start.20 = (f32[16,1,256]{2,1,0:T(1,128)S(1)}, f32[16,1,256]{2,1,0:T(1,128)S(1)}, u32[]{:S(2)}, u32[]{:S(2)}) collective-permute-start(f32[16,1,256]{2,1,0:T(1,128)S(1)} %get-tuple-element.46), channel_id=1, source_target_pairs={{0,16},{16,32},{32,48},{48,64},{64,80},{80,96},{96,112},{112,128},... | collective-permute-start | bytes 49160 | tf_op jit(solution)/shard_map/ppermute | solution.py:20
  104.9 4.6 %collective-permute-start.21 = (f32[16,1,256]{2,1,0:T(1,128)S(1)}, f32[16,1,256]{2,1,0:T(1,128)S(1)}, u32[]{:S(2)}, u32[]{:S(2)}) collective-permute-start(f32[16,1,256]{2,1,0:T(1,128)S(1)} %get-tuple-element.47), channel_id=1, source_target_pairs={{16,0},{32,16},{48,32},{64,48},{80,64},{96,80},{112,96},{128,112},... | collective-permute-start | bytes 49160 | tf_op jit(solution)/shard_map/ppermute | solution.py:21
  109.6 7.9 %collective-permute-start.22 = (f32[16,18,1]{2,1,0:T(8,128)S(1)}, f32[16,18,1]{2,1,0:T(8,128)S(1)}, u32[]{:S(2)}, u32[]{:S(2)}) collective-permute-start(f32[16,18,1]{2,1,0:T(8,128)S(1)} %get-tuple-element.29), channel_id=1, source_target_pairs={{0,1},{1,2},{2,3},{3,4},{4,5},{5,6},{6,7},{7,8},{8,9},{9,10},{10,1... | collective-permute-start | bytes 3464 | tf_op jit(solution)/shard_map/ppermute | solution.py:20
  114.4 7.6 %collective-permute-start.23 = (f32[16,18,1]{2,1,0:T(8,128)S(1)}, f32[16,18,1]{2,1,0:T(8,128)S(1)}, u32[]{:S(2)}, u32[]{:S(2)}) collective-permute-start(f32[16,18,1]{2,1,0:T(8,128)S(1)} %get-tuple-element.28), channel_id=1, source_target_pairs={{1,0},{2,1},{3,2},{4,3},{5,4},{6,5},{7,6},{8,7},{9,8},{10,9},{11,1... | collective-permute-start | bytes 3464 | tf_op jit(solution)/shard_map/ppermute | solution.py:21
  122.9 6.9 %collective-permute-start.24 = (f32[16,1,256]{2,1,0:T(1,128)S(1)}, f32[16,1,256]{2,1,0:T(1,128)S(1)}, u32[]{:S(2)}, u32[]{:S(2)}) collective-permute-start(f32[16,1,256]{2,1,0:T(1,128)S(1)} %get-tuple-element.44), channel_id=1, source_target_pairs={{0,16},{16,32},{32,48},{48,64},{64,80},{80,96},{96,112},{112,128},... | collective-permute-start | bytes 49160 | tf_op jit(solution)/shard_map/ppermute | solution.py:20
  127.9 4.2 %collective-permute-start.25 = (f32[16,1,256]{2,1,0:T(1,128)S(1)}, f32[16,1,256]{2,1,0:T(1,128)S(1)}, u32[]{:S(2)}, u32[]{:S(2)}) collective-permute-start(f32[16,1,256]{2,1,0:T(1,128)S(1)} %get-tuple-element.45), channel_id=1, source_target_pairs={{16,0},{32,16},{48,32},{64,48},{80,64},{96,80},{112,96},{128,112},... | collective-permute-start | bytes 49160 | tf_op jit(solution)/shard_map/ppermute | solution.py:21
  132.2 8.3 %collective-permute-start.26 = (f32[16,18,1]{2,1,0:T(8,128)S(1)}, f32[16,18,1]{2,1,0:T(8,128)S(1)}, u32[]{:S(2)}, u32[]{:S(2)}) collective-permute-start(f32[16,18,1]{2,1,0:T(8,128)S(1)} %get-tuple-element.27), channel_id=1, source_target_pairs={{0,1},{1,2},{2,3},{3,4},{4,5},{5,6},{6,7},{7,8},{8,9},{9,10},{10,1... | collective-permute-start | bytes 3464 | tf_op jit(solution)/shard_map/ppermute | solution.py:20
  137.4 7.6 %collective-permute-start.27 = (f32[16,18,1]{2,1,0:T(8,128)S(1)}, f32[16,18,1]{2,1,0:T(8,128)S(1)}, u32[]{:S(2)}, u32[]{:S(2)}) collective-permute-start(f32[16,18,1]{2,1,0:T(8,128)S(1)} %get-tuple-element.26), channel_id=1, source_target_pairs={{1,0},{2,1},{3,2},{4,3},{5,4},{6,5},{7,6},{8,7},{9,8},{10,9},{11,1... | collective-permute-start | bytes 3464 | tf_op jit(solution)/shard_map/ppermute | solution.py:21
  146.0 6.6 %collective-permute-start.28 = (f32[16,1,256]{2,1,0:T(1,128)S(1)}, f32[16,1,256]{2,1,0:T(1,128)S(1)}, u32[]{:S(2)}, u32[]{:S(2)}) collective-permute-start(f32[16,1,256]{2,1,0:T(1,128)S(1)} %get-tuple-element.42), channel_id=1, source_target_pairs={{0,16},{16,32},{32,48},{48,64},{64,80},{80,96},{96,112},{112,128},... | collective-permute-start | bytes 49160 | tf_op jit(solution)/shard_map/ppermute | solution.py:20
  150.6 4.4 %collective-permute-start.29 = (f32[16,1,256]{2,1,0:T(1,128)S(1)}, f32[16,1,256]{2,1,0:T(1,128)S(1)}, u32[]{:S(2)}, u32[]{:S(2)}) collective-permute-start(f32[16,1,256]{2,1,0:T(1,128)S(1)} %get-tuple-element.43), channel_id=1, source_target_pairs={{16,0},{32,16},{48,32},{64,48},{80,64},{96,80},{112,96},{128,112},... | collective-permute-start | bytes 49160 | tf_op jit(solution)/shard_map/ppermute | solution.py:21
  155.3 7.1 %collective-permute-start.30 = (f32[16,18,1]{2,1,0:T(8,128)S(1)}, f32[16,18,1]{2,1,0:T(8,128)S(1)}, u32[]{:S(2)}, u32[]{:S(2)}) collective-permute-start(f32[16,18,1]{2,1,0:T(8,128)S(1)} %get-tuple-element.25), channel_id=1, source_target_pairs={{0,1},{1,2},{2,3},{3,4},{4,5},{5,6},{6,7},{7,8},{8,9},{9,10},{10,1... | collective-permute-start | bytes 3464 | tf_op jit(solution)/shard_map/ppermute | solution.py:20
  159.2 7.6 %collective-permute-start.31 = (f32[16,18,1]{2,1,0:T(8,128)S(1)}, f32[16,18,1]{2,1,0:T(8,128)S(1)}, u32[]{:S(2)}, u32[]{:S(2)}) collective-permute-start(f32[16,18,1]{2,1,0:T(8,128)S(1)} %get-tuple-element.24), channel_id=1, source_target_pairs={{1,0},{2,1},{3,2},{4,3},{5,4},{6,5},{7,6},{8,7},{9,8},{10,9},{11,1... | collective-permute-start | bytes 3464 | tf_op jit(solution)/shard_map/ppermute | solution.py:21
  167.2 15.5 %copy-start.4 = (s32[16,256]{1,0:T(8,128)S(1)}, s32[16,256]{1,0:T(8,128)}, u32[]{:S(2)}) copy-start(s32[16,256]{1,0:T(8,128)} %param.6) | copy-start | bytes 49156
  167.9 21.7 %copy-start.1 = (f32[16,16,256]{2,1,0:T(8,128)}, f32[16,16,256]{2,1,0:T(8,128)S(1)}, u32[]{:S(2)}) copy-start(f32[16,16,256]{2,1,0:T(8,128)S(1)} %fusion.23) | copy-start | bytes 786436
  167.9 6.6 %collective-permute-start.32 = (f32[16,1,256]{2,1,0:T(1,128)S(1)}, f32[16,1,256]{2,1,0:T(1,128)S(1)}, u32[]{:S(2)}, u32[]{:S(2)}) collective-permute-start(f32[16,1,256]{2,1,0:T(1,128)S(1)} %get-tuple-element.40), channel_id=1, source_target_pairs={{0,16},{16,32},{32,48},{48,64},{64,80},{80,96},{96,112},{112,128},... | collective-permute-start | bytes 49160 | tf_op jit(solution)/shard_map/ppermute | solution.py:20
  172.6 4.4 %collective-permute-start.33 = (f32[16,1,256]{2,1,0:T(1,128)S(1)}, f32[16,1,256]{2,1,0:T(1,128)S(1)}, u32[]{:S(2)}, u32[]{:S(2)}) collective-permute-start(f32[16,1,256]{2,1,0:T(1,128)S(1)} %get-tuple-element.41), channel_id=1, source_target_pairs={{16,0},{32,16},{48,32},{64,48},{80,64},{96,80},{112,96},{128,112},... | collective-permute-start | bytes 49160 | tf_op jit(solution)/shard_map/ppermute | solution.py:21
  177.2 7.1 %collective-permute-start.34 = (f32[16,18,1]{2,1,0:T(8,128)S(1)}, f32[16,18,1]{2,1,0:T(8,128)S(1)}, u32[]{:S(2)}, u32[]{:S(2)}) collective-permute-start(f32[16,18,1]{2,1,0:T(8,128)S(1)} %get-tuple-element.23), channel_id=1, source_target_pairs={{0,1},{1,2},{2,3},{3,4},{4,5},{5,6},{6,7},{7,8},{8,9},{9,10},{10,1... | collective-permute-start | bytes 3464 | tf_op jit(solution)/shard_map/ppermute | solution.py:20
  181.2 7.6 %collective-permute-start.35 = (f32[16,18,1]{2,1,0:T(8,128)S(1)}, f32[16,18,1]{2,1,0:T(8,128)S(1)}, u32[]{:S(2)}, u32[]{:S(2)}) collective-permute-start(f32[16,18,1]{2,1,0:T(8,128)S(1)} %get-tuple-element.22), channel_id=1, source_target_pairs={{1,0},{2,1},{3,2},{4,3},{5,4},{6,5},{7,6},{8,7},{9,8},{10,9},{11,1... | collective-permute-start | bytes 3464 | tf_op jit(solution)/shard_map/ppermute | solution.py:21
  189.6 50.4 %copy-start.3 = (f32[16,16,256]{2,1,0:T(8,128)}, f32[16,16,256]{2,1,0:T(8,128)S(1)}, u32[]{:S(2)}) copy-start(f32[16,16,256]{2,1,0:T(8,128)S(1)} %fusion.3) | copy-start | bytes 786436
  189.7 33.9 %copy-start.5 = (s32[16]{0:T(128)S(1)}, s32[16]{0:T(128)}, u32[]{:S(2)}) copy-start(s32[16]{0:T(128)} %param.7) | copy-start | bytes 196
  190.1 5.5 %collective-permute-start.36 = (f32[16,16,256]{2,1,0:T(8,128)S(1)}, f32[16,16,256]{2,1,0:T(8,128)S(1)}, u32[]{:S(2)}, u32[]{:S(2)}) collective-permute-start(f32[16,16,256]{2,1,0:T(8,128)S(1)} %convolution_bitcast_fusion), channel_id=1, source_target_pairs={{0,16},{16,0},{32,48},{48,32},{64,80},{80,64},{96,112},{112,96},{1... | collective-permute-start | bytes 786440 | tf_op jit(solution)/shard_map/ppermute | solution.py:27
  195.7 13.9 %collective-permute-start.37 = (f32[16,16,256]{2,1,0:T(8,128)S(1)}, f32[16,16,256]{2,1,0:T(8,128)S(1)}, u32[]{:S(2)}, u32[]{:S(2)}) collective-permute-start(f32[16,16,256]{2,1,0:T(8,128)S(1)} %select_multiply_fusion.4), channel_id=1, source_target_pairs={{0,32},{16,48},{32,0},{48,16},{64,96},{80,112},{96,64},{112,80},{1... | collective-permute-start | bytes 786440 | tf_op jit(solution)/shard_map/ppermute | solution.py:27
  209.6 11.4 %collective-permute-start.38 = (f32[16,16,256]{2,1,0:T(8,128)S(1)}, f32[16,16,256]{2,1,0:T(8,128)S(1)}, u32[]{:S(2)}, u32[]{:S(2)}) collective-permute-start(f32[16,16,256]{2,1,0:T(8,128)S(1)} %select_multiply_fusion.3), channel_id=1, source_target_pairs={{0,64},{16,80},{32,96},{48,112},{64,0},{80,16},{96,32},{112,48},{1... | collective-permute-start | bytes 786440 | tf_op jit(solution)/shard_map/ppermute | solution.py:27
  221.1 9.0 %collective-permute-start.39 = (f32[16,16,256]{2,1,0:T(8,128)S(1)}, f32[16,16,256]{2,1,0:T(8,128)S(1)}, u32[]{:S(2)}, u32[]{:S(2)}) collective-permute-start(f32[16,16,256]{2,1,0:T(8,128)S(1)} %select_multiply_fusion.2), channel_id=1, source_target_pairs={{0,128},{16,144},{32,160},{48,176},{64,192},{80,208},{96,224},{112... | collective-permute-start | bytes 786440 | tf_op jit(solution)/shard_map/ppermute | solution.py:27
  230.2 9.8 %collective-permute-start.40 = (f32[16,16,256]{2,1,0:T(8,128)S(1)}, f32[16,16,256]{2,1,0:T(8,128)S(1)}, u32[]{:S(2)}, u32[]{:S(2)}) collective-permute-start(f32[16,16,256]{2,1,0:T(8,128)S(1)} %select_multiply_fusion.1), channel_id=1, source_target_pairs={{0,256},{16,272},{32,288},{48,304},{64,320},{80,336},{96,352},{112... | collective-permute-start | bytes 786440 | tf_op jit(solution)/shard_map/ppermute | solution.py:27
